TPU v7x, 128 devices: a whole 4x4x4 slice. The times are simulated.
128 devices in a mesh: rock: 8 (over y, core), plane: 16 (over z, x).
Axes of the slice: x: 4, y: 4, z: 4, core: 2. Of those that a mesh axis runs over, the one named last changes fastest.
Arguments:
- rock_state: float32 [36, 262144], P(None, ('rock', 'plane')), may hold values from -6 to 6
- jacobian: float32 [262144], P(('rock', 'plane')), may hold values from 0.5 to 2
- stiffness: float32 [36, 36], replicated, may hold values from -1 to 1
- trace_map: float32 [36, 36], replicated, may hold values from -1 to 1
- lift_map: float32 [36, 36], replicated, may hold values from -1 to 1
- neighbor_elem: int32 [4, 262144], P(None, ('rock', 'plane')), may hold values from 0 to 4095
- neighbor_face: int32 [4, 262144], P(None, ('rock', 'plane')), may hold values from 0 to 3
- send_elem: int32 [2, 131072], P(None, ('rock', 'plane')), may hold values from 0 to 2047
- opening_dir: float32 [36], replicated, may hold values from -1 to 1
- traction_dir: float32 [36], replicated, may hold values from -4 to 4
- face_elem: int32 [1048576], P(('rock', 'plane')), may hold values from 0 to 2047
- face_tile: int32 [1048576], P(('rock', 'plane')), may hold values from 0 to 15, as said below
- face_cell: int32 [1048576], P(('rock', 'plane')), may hold values from 0 to 16383
- face_count: int32 [128], P(('rock', 'plane')), may hold values from 2048 to 8192, as said below
- pressure: float32 [8, 32, 8192], P('rock', 'plane'), may hold values from -6 to 6
- base_aperture: float32 [8, 32, 8192], P('rock', 'plane'), may hold values from 0.4 to 1.2
- injection: float32 [8, 32, 8192], P('rock', 'plane'), may hold values from -6 to 6
Outputs:
- new_state: float32 [36, 262144], P(None, ('rock', 'plane'))
- new_pressure: float32 [8, 32, 8192], P('rock', 'plane')
- aperture: float32 [8, 32, 8192], P('rock', 'plane')
Inputs may be any that keep to these rules, and one draw needn't show every extreme that they name: `face_tile`: each partition's 8192 slots name every tile exactly 512 times. `face_count`: some partition has all slots live.
All inputs are finite; a program needn't handle non-finite values.
Results may differ from a plain program's by a relative error of at most 0.00005.
Values sent between devices are 32-bit elements; how exact they have to be, the bound alone decides.
A program may use at most 64 MiB of HBM per device.

v0:
```python
import jax
import jax.numpy as jnp
from jax import lax
from jax.sharding import PartitionSpec as P

STEP = 0.25
RATE = 0.35


def extended_2(block, sides, width):
    for axis, dim in sides:
        count = lax.axis_size(axis)
        forward = [(i, i + 1) for i in range(count - 1)]
        backward = [(target, source) for source, target in forward]
        low = lax.ppermute(
            lax.slice_in_dim(block, block.shape[dim] - width, None, axis=dim), axis, forward
        )
        high = lax.ppermute(lax.slice_in_dim(block, 0, width, axis=dim), axis, backward)
        block = jnp.concatenate([low, block, high], axis=dim)
    return block


def neighbor_jumps(traces, lower_rim, upper_rim, near_elem, near_face):
    trace_pool = jnp.concatenate([traces, lower_rim, upper_rim], axis=1)
    width = traces.shape[0] // 4
    elements = traces.shape[1]
    pool_columns = trace_pool.shape[1]
    folded = (
        trace_pool.reshape(4, width, pool_columns)
        .transpose(1, 0, 2)
        .reshape(width, 4 * pool_columns)
    )
    flat_index = (near_face * pool_columns + near_elem).reshape(-1)
    chosen = (
        folded[:, flat_index]
        .reshape(width, 4, elements)
        .transpose(1, 0, 2)
        .reshape(4 * width, elements)
    )
    return chosen - traces


def flux_sum(padded_p, padded_c):
    rows = padded_p.shape[0] - 2
    columns = padded_p.shape[1] - 2
    centre_p = padded_p[1 : rows + 1, 1 : columns + 1]
    centre_c = padded_c[1 : rows + 1, 1 : columns + 1]
    total = jnp.zeros((rows, columns), jnp.float32)
    for offset_row, offset_col in ((0, 1), (2, 1), (1, 0), (1, 2)):
        other_p = padded_p[offset_row : offset_row + rows, offset_col : offset_col + columns]
        other_c = padded_c[offset_row : offset_row + rows, offset_col : offset_col + columns]
        link = 2.0 * centre_c * other_c / (centre_c + other_c)
        total = total + link * (other_p - centre_p)
    return total


def elastic_step(
    state, jacobian, stiffness, trace_map, lift_map, neighbor_elem, neighbor_face, send_elem
):
    traces = jnp.dot(trace_map, state, precision=lax.Precision.HIGHEST)
    halo_rows = send_elem.shape[1]
    outgoing = jnp.concatenate([traces[:, send_elem[0]], traces[:, send_elem[1]]], axis=1)
    extended = extended_2(outgoing, ((("rock", "plane"), 1),), halo_rows)
    lower_rim = extended[:, :halo_rows]
    upper_rim = extended[:, 3 * halo_rows :]
    jumps = neighbor_jumps(traces, lower_rim, upper_rim, neighbor_elem, neighbor_face)
    change = jnp.dot(stiffness, state, precision=lax.Precision.HIGHEST) + jnp.dot(
        lift_map, jumps, precision=lax.Precision.HIGHEST
    )
    return state + STEP * jacobian[None, :] * change


def shards(
    rock_state,
    jacobian,
    stiffness,
    trace_map,
    lift_map,
    neighbor_elem,
    neighbor_face,
    send_elem,
    opening_dir,
    traction_dir,
    face_elem,
    face_tile,
    face_cell,
    face_count,
    pressure,
    base_aperture,
    injection,
):
    state = elastic_step(
        rock_state,
        jacobian,
        stiffness,
        trace_map,
        lift_map,
        neighbor_elem,
        neighbor_face,
        send_elem,
    )
    tiles = lax.axis_size("plane")
    slot_total = face_cell.shape[0]
    rows = pressure.shape[1]
    columns = pressure.shape[2]
    tile_cells = rows * columns
    grid_cell = face_tile * tile_cells + face_cell
    live = jnp.arange(slot_total, dtype=jnp.int32) < face_count[0]
    scores = jnp.dot(opening_dir, state, precision=lax.Precision.HIGHEST)
    openings = jnp.where(live, 0.2 * jax.nn.softplus(scores[face_elem]), 0.0)
    field = jnp.zeros((tiles * tile_cells,), jnp.float32).at[grid_cell].add(openings)
    arrived = lax.psum_scatter(field, "plane", scatter_dimension=0, tiled=True)
    aperture = base_aperture[0] + arrived.reshape(rows, columns)
    conduct = aperture * aperture * aperture / 12.0
    stacked = jnp.stack([pressure[0], conduct])
    extended = extended_2(stacked, (("plane", 1),), 1)
    padded = jnp.pad(extended, ((0, 0), (0, 0), (1, 1)))
    new_pressure = pressure[0] + RATE * (flux_sum(padded[0], padded[1]) + injection[0])
    whole = lax.all_gather(new_pressure.reshape(-1), "plane", axis=0, tiled=True)
    face_pressure = whole[grid_cell]
    face_pressure = jnp.where(live, face_pressure, 0.0)
    load = jnp.zeros((state.shape[1],), jnp.float32).at[face_elem].add(face_pressure)
    loaded = state + STEP * (jacobian * load)[None, :] * traction_dir[:, None]
    new_state = elastic_step(
        loaded, jacobian, stiffness, trace_map, lift_map, neighbor_elem, neighbor_face, send_elem
    )
    return (new_state, new_pressure[None], aperture[None])


def solution(mesh):
    return jax.shard_map(
        shards,
        mesh=mesh,
        in_specs=(
            P(None, ("rock", "plane")),
            P(("rock", "plane")),
            P(),
            P(),
            P(),
            P(None, ("rock", "plane")),
            P(None, ("rock", "plane")),
            P(None, ("rock", "plane")),
            P(),
            P(),
            P(("rock", "plane")),
            P(("rock", "plane")),
            P(("rock", "plane")),
            P(("rock", "plane")),
            P("rock", "plane", None),
            P("rock", "plane", None),
            P("rock", "plane", None),
        ),
        out_specs=(P(None, ("rock", "plane")), P("rock", "plane", None), P("rock", "plane", None)),
        check_vma=False,
    )
```

profile of v0, /device:TPU:1, one launch (start us, length us, event | category | flops | bytes accessed | tf_op | source)
XLA Modules:
  0.0 512.1 jit_solution(16181090862808466744)
XLA Ops:
  7.9 1.4 fusion.36
  9.7 0.8 compare_select_fusion.5
  10.5 2.8 gather_fusion
  13.5 3.9 collective-permute-start
  17.4 2.8 gather_fusion.1
  20.5 7.2 %collective-permute-start.1 = (f32[36,1024]{1,0:T(8,128)S(1)}, f32[36,1024]{1,0:T(8,128)S(1)}, u32[]{:S(2)}, u32[]{:S(2)}) collective-permute-start(f32[36,1024]{1,0:T(8,128)S(1)} %bitcast.85), channel_id=1, source_target_pairs={{1,0},{2,1},{3,2},{4,3},{5,4},{6,5},{7,6},{8,7},{9,8},{10,9},{11,1... | collective-permute-start | bytes 442376 | tf_op jit(solution)/shard_map/ppermute | solution.py:18
  29.0 0.9 collective-permute-done.1
  30.1 4.7 copy.48
  34.8 31.2 %gather_fusion.2 = f32[8192,9]{1,0:T(8,128)} fusion(f32[9,16384]{0,1:T(8,128)} %bitcast.74, s32[8192]{0:T(1024)S(1)} %broadcast_clamp_fusion.2), kind=kCustom, calls=%fused_computation.2 | custom fusion | bytes 622592 | tf_op jit(solution)/shard_map/gather | solution.py:35
  66.0 2.9 copy.49
  69.8 45.5 %gather_fusion.3 = f32[8192]{0:T(1024)S(1)} fusion(f32[2048]{0:T(1024)S(1)} %bitcast.72, s32[8192]{0:T(1024)S(1)} %get-tuple-element.11), kind=kCustom, calls=%fused_computation.3 | custom fusion | bytes 98304 | tf_op jit(solution)/shard_map/gather | solution.py:110
  115.3 44.2 %scatter_custom_fusion = f32[262144]{0:T(1024)} fusion(s32[8192]{0:T(1024)S(1)} %get-tuple-element.4, f32[8192]{0:T(1024)S(1)} %fusion.29, f32[]{:T(128)} %constant.16.clone.1), kind=kCustom, calls=%fused_computation.21 | custom fusion | flops 8192 | bytes 1048580 | tf_op jit(solution)/shard_map/scatter-add | solution.py:111
  160.9 87.9 %all-reduce.4.cloned.1.call-done = f32[262144]{0:T(1024)} async-done(((f32[262144]{0:T(1024)}), f32[262144]{0:T(1024)}) %all-reduce.4.cloned.1.call-update) | async-done | bytes 1048592
  248.7 0.8 dynamic-slice.1
  249.6 0.7 fusion.16
  250.4 2.6 collective-permute-start.2
  253.1 1.3 collective-permute-start.3
  254.4 3.7 collective-permute-done.3
  258.6 0.6 bitcast_add_fusion
  259.2 0.6 copy.57
  259.9 47.1 %all-gather.2.cloned.1.call-done = f32[262144]{0:T(1024)} async-done(((f32[16384]{0:T(1024)}), f32[262144]{0:T(1024)}) %all-gather.2.cloned.1.call-update) | async-done | bytes 1048592 | tf_op jit(solution)/shard_map/all_gather | solution.py:119
  307.0 96.4 %gather_fusion.4 = f32[8192]{0:T(1024)S(1)} fusion(f32[262144]{0:T(1024)} %all-gather.2.cloned.1.call-done, s32[8192]{0:T(1024)S(1)} %get-tuple-element.3), kind=kCustom, calls=%fused_computation.4 | custom fusion | bytes 98304 | tf_op jit(solution)/shard_map/gather | solution.py:120
  403.4 43.5 %scatter_custom_fusion.1 = f32[2048]{0:T(1024)S(1)} fusion(s32[8192]{0:T(1024)S(1)} %get-tuple-element.12, f32[8192]{0:T(1024)S(1)} %fusion.30, f32[]{:T(128)} %constant.16.clone.1), kind=kCustom, calls=%fused_computation.77 | custom fusion | flops 8192 | bytes 8196 | tf_op jit(solution)/shard_map/scatter-add | solution.py:122
  447.9 2.8 gather_fusion.5
  450.7 2.8 gather_fusion.6
  453.7 3.1 collective-permute-start.4
  457.0 5.8 %collective-permute-start.5 = (f32[36,1024]{1,0:T(8,128)S(1)}, f32[36,1024]{1,0:T(8,128)S(1)}, u32[]{:S(2)}, u32[]{:S(2)}) collective-permute-start(f32[36,1024]{1,0:T(8,128)S(1)} %bitcast.87), channel_id=1, source_target_pairs={{1,0},{2,1},{3,2},{4,3},{5,4},{6,5},{7,6},{8,7},{9,8},{10,9},{11,1... | collective-permute-start | bytes 442376 | tf_op jit(solution)/shard_map/ppermute | solution.py:18
  463.7 1.4 collective-permute-done.5
  465.2 4.7 copy.54
  469.9 31.2 %gather_fusion.7 = f32[8192,9]{1,0:T(8,128)} fusion(f32[9,16384]{0,1:T(8,128)} %bitcast.73, s32[8192]{0:T(1024)S(1)} %broadcast_clamp_fusion.2), kind=kCustom, calls=%fused_computation.7 | custom fusion | bytes 622592 | tf_op jit(solution)/shard_map/gather | solution.py:35
  501.1 2.8 copy.55
  504.0 1.2 fusion.5
  (75 shorter events, 6.6 us)
Async XLA Ops:
  7.2 0.7 copy-start
  7.2 20.6 %copy-start.1 = (f32[36,2048]{1,0:T(8,128)S(1)}, f32[36,2048]{1,0:T(8,128)}, u32[]{:S(2)}) copy-start(f32[36,2048]{1,0:T(8,128)} %param.17) | copy-start | bytes 884740
  7.2 20.5 %copy-start.8 = (s32[4,2048]{1,0:T(4,128)S(1)}, s32[4,2048]{1,0:T(4,128)}, u32[]{:S(2)}) copy-start(s32[4,2048]{1,0:T(4,128)} %param.22) | copy-start | bytes 98308
  7.2 20.5 %copy-start.9 = (s32[4,2048]{1,0:T(4,128)S(1)}, s32[4,2048]{1,0:T(4,128)}, u32[]{:S(2)}) copy-start(s32[4,2048]{1,0:T(4,128)} %param.23) | copy-start | bytes 98308
  7.2 20.6 %copy-start.4 = (f32[36,36]{1,0:T(8,128)S(1)}, f32[36,36]{1,0:T(8,128)}, u32[]{:S(2)}) copy-start(f32[36,36]{1,0:T(8,128)} %param.19) | copy-start | bytes 15556
  7.2 21.0 %copy-start.10 = (s32[8192]{0:T(1024)S(1)}, s32[8192]{0:T(1024)}, u32[]{:S(2)}) copy-start(s32[8192]{0:T(1024)} %param.27) | copy-start | bytes 98308
  7.2 21.7 %copy-start.13 = (s32[8192]{0:T(1024)S(1)}, s32[8192]{0:T(1024)}, u32[]{:S(2)}) copy-start(s32[8192]{0:T(1024)} %param.28) | copy-start | bytes 98308
  7.2 21.7 %copy-start.12 = (s32[8192]{0:T(1024)S(1)}, s32[8192]{0:T(1024)}, u32[]{:S(2)}) copy-start(s32[8192]{0:T(1024)} %param.29) | copy-start | bytes 98308
  7.3 21.7 %copy-start.11 = (f32[2048]{0:T(1024)S(1)}, f32[2048]{0:T(1024)}, u32[]{:S(2)}) copy-start(f32[2048]{0:T(1024)} %param.18) | copy-start | bytes 24580
  7.3 241.5 %all-reduce.4.cloned.1.call-start = ((), (), s32[]{:S(2)}) async-start(), calls=%async_computation.1 | async-start | bytes 2097152
  13.5 15.5 %collective-permute-start = (f32[36,1024]{1,0:T(8,128)S(1)}, f32[36,1024]{1,0:T(8,128)S(1)}, u32[]{:S(2)}, u32[]{:S(2)}) collective-permute-start(f32[36,1024]{1,0:T(8,128)S(1)} %bitcast.84), channel_id=1, source_target_pairs={{0,1},{1,2},{2,3},{3,4},{4,5},{5,6},{6,7},{7,8},{8,9},{9,10},{10,1... | collective-permute-start | bytes 442376 | tf_op jit(solution)/shard_map/ppermute | solution.py:15
  20.5 9.5 %collective-permute-start.1 = (f32[36,1024]{1,0:T(8,128)S(1)}, f32[36,1024]{1,0:T(8,128)S(1)}, u32[]{:S(2)}, u32[]{:S(2)}) collective-permute-start(f32[36,1024]{1,0:T(8,128)S(1)} %bitcast.85), channel_id=1, source_target_pairs={{1,0},{2,1},{3,2},{4,3},{5,4},{6,5},{7,6},{8,7},{9,8},{10,9},{11,1... | collective-permute-start | bytes 442376 | tf_op jit(solution)/shard_map/ppermute | solution.py:18
  34.8 34.2 %copy-start.5 = (f32[36,36]{1,0:T(8,128)S(1)}, f32[36,36]{1,0:T(8,128)}, u32[]{:S(2)}) copy-start(f32[36,36]{1,0:T(8,128)} %param.21) | copy-start | bytes 15556
  66.0 3.4 copy-start.15
  69.7 89.9 %copy-start.16 = (u32[128]{0:T(128)S(1)}, u32[128]{0:T(128)}, u32[]{:S(2)}) copy-start(u32[128]{0:T(128)} %constant.39) | copy-start | bytes 1540
  69.7 179.9 %copy-start.6 = (f32[1,2,8192]{2,1,0:T(2,128)S(1)}, f32[1,2,8192]{2,1,0:T(2,128)}, u32[]{:S(2)}) copy-start(f32[1,2,8192]{2,1,0:T(2,128)} %param.32) | copy-start | bytes 196612
  69.7 180.6 %copy-start.2 = (f32[1,2,8192]{2,1,0:T(2,128)S(1)}, f32[1,2,8192]{2,1,0:T(2,128)}, u32[]{:S(2)}) copy-start(f32[1,2,8192]{2,1,0:T(2,128)} %param.31) | copy-start | bytes 196612
  69.8 188.8 %copy-start.7 = (f32[1,2,8192]{2,1,0:T(2,128)S(1)}, f32[1,2,8192]{2,1,0:T(2,128)}, u32[]{:S(2)}) copy-start(f32[1,2,8192]{2,1,0:T(2,128)} %param.33) | copy-start | bytes 196612
  159.6 147.4 %all-gather.2.cloned.1.call-start = ((), (), s32[]{:S(2)}) async-start(), calls=%async_computation | async-start | bytes 1114112 | tf_op jit(solution)/shard_map/all_gather | solution.py:119
  250.4 3.9 collective-permute-start.2
  253.1 5.0 collective-permute-start.3
  259.2 144.2 %copy-start.3 = (f32[2,8192]{1,0:T(2,128)}, f32[2,8192]{1,0:T(2,128)S(1)}, u32[]{:S(2)}) copy-start(f32[2,8192]{1,0:T(2,128)S(1)} %bitcast_add_fusion) | copy-start | bytes 196612
  307.0 140.0 %copy-start.14 = (f32[36]{0:T(128)S(1)}, f32[36]{0:T(128)}, u32[]{:S(2)}) copy-start(f32[36]{0:T(128)} %param.26) | copy-start | bytes 436
  453.7 10.0 %collective-permute-start.4 = (f32[36,1024]{1,0:T(8,128)S(1)}, f32[36,1024]{1,0:T(8,128)S(1)}, u32[]{:S(2)}, u32[]{:S(2)}) collective-permute-start(f32[36,1024]{1,0:T(8,128)S(1)} %bitcast.86), channel_id=1, source_target_pairs={{0,1},{1,2},{2,3},{3,4},{4,5},{5,6},{6,7},{7,8},{8,9},{9,10},{10,1... | collective-permute-start | bytes 442376 | tf_op jit(solution)/shard_map/ppermute | solution.py:15
  457.0 8.0 %collective-permute-start.5 = (f32[36,1024]{1,0:T(8,128)S(1)}, f32[36,1024]{1,0:T(8,128)S(1)}, u32[]{:S(2)}, u32[]{:S(2)}) collective-permute-start(f32[36,1024]{1,0:T(8,128)S(1)} %bitcast.87), channel_id=1, source_target_pairs={{1,0},{2,1},{3,2},{4,3},{5,4},{6,5},{7,6},{8,7},{9,8},{10,9},{11,1... | collective-permute-start | bytes 442376 | tf_op jit(solution)/shard_map/ppermute | solution.py:18
Sparse Core Ops, SparseCore 0:
  159.7 89.0 all-reduce.3
  260.0 46.9 all-gather.1
where the time goes:
time: 518 us; the launch traced here: 512 us
  local copies, waits for them, and re-layouts  235 us (45%)
  waiting for transfers between devices  141 us (27%)
  other arithmetic  90.6 us (17%)
  starting transfers between devices  24 us (5%)
  between operations  15.9 us (3%)
    gather x1, local copies, waits for them, and re-layouts, shards(): face_pressure = whole[grid_cell]  96.4 us
    unnamed x3, waiting for transfers between devices  87.9 us
    gather x2, local copies, waits for them, and re-layouts, neighbor_jumps(): folded[:, flat_index].reshape(width, 4, elements).transpose(1, 0, 2)  62.5 us
    all_gather x1, waiting for transfers between devices, shards(): lax.all_gather(new_pressure.reshape(-1), 'plane', axis=0, tiled=True)  47.1 us
    gather x1, local copies, waits for them, and re-layouts, shards(): openings = jnp.where(live, 0.2 * jax.nn.softplus(scores[face_elem]), 0.0)  45.5 us
    scatter-add x1, other arithmetic, shards(): jnp.zeros((tiles * tile_cells,), jnp.float32).at[grid_cell].add(openings)  44.2 us
    scatter-add x1, other arithmetic, shards(): jnp.zeros((state.shape[1],), jnp.float32).at[face_elem].add(face_pressure)  43.5 us
    ppermute x3, starting transfers between devices, extended_2(): lax.ppermute(lax.slice_in_dim(block, 0, width, axis=dim), axis, backward)  14.3 us
  transfers between devices with their start and end apart: 8, of which 6 were waited for; matrix products, arithmetic and copies ran while one was open for 1% of the time, Pallas kernels for 0%

commit v1 on v0

v1 whole, which is shorter than its diff:
```python
import jax
import jax.numpy as jnp
from jax import lax
from jax.experimental import pallas as pl
from jax.experimental.pallas import tpu as pltpu
from jax.sharding import PartitionSpec as P

STEP = 0.25
RATE = 0.35
F32 = jnp.float32
BF16 = jnp.bfloat16
I32 = jnp.int32
MESH = pl.DeviceIdType.MESH
Q = 36
QP = 40
QB = 48
ELEMS = 2048
HALO = 1024
SLOTS = 8192
TILES = 16
PARTS = 128


def dot(a, b):
    return jnp.dot(a, b, preferred_element_type=F32)


def dot_nt(a, b):
    return lax.dot_general(a, b, (((1,), (1,)), ((), ())), preferred_element_type=F32)


def exact_dot(a, b):
    return jnp.dot(a, b, preferred_element_type=F32, precision=lax.Precision.HIGHEST)


def split(x):
    high = x.astype(BF16)
    return high, (x - high.astype(F32)).astype(BF16)


def iota(shape, dim):
    return lax.broadcasted_iota(I32, shape, dim)


def ones_where(mask):
    return jnp.where(mask, 1.0, 0.0).astype(F32)


def lanes(chunk, width=128):
    return pl.ds(pl.multiple_of(chunk * width, width), width)


def padded(x, rows):
    return jnp.concatenate([x, jnp.zeros((rows - x.shape[0],) + x.shape[1:], x.dtype)], axis=0)


def column(row):
    wide = jnp.broadcast_to(row, (QP, Q))
    eye = iota((QP, Q), 0) == iota((QP, Q), 1)
    return jnp.sum(jnp.where(eye, wide, 0.0), axis=1, keepdims=True)


def kernel(
    state_ref, jac_ref, stiff_ref, tmap_ref, lift_ref, nel_ref, nfa_ref, send_ref, odir_ref, tdir_ref,
    fel_ref, ftile_ref, fcell_ref, fcount_ref, press_ref, base_ref, inj_ref,
    new_state_ref, new_press_ref, aper_ref,
    s1, table, hot, send_hot, xh, xl, ww, tw, uu, out1, out2, rim1, rim2, wout, wrim,
    va, vb, elem_hot, elem_row, cells_out, cells_in, open_out, open_in, press_out, press_in,
    slot_tab, cell_hi, cell_lo, val, cond, edge_out, edge_in, edge_wide, change1, lane_row,
    halo_send, halo_recv, cell_send, cell_recv, open_send, open_recv, pr_send, pr_recv, edge_send, edge_recv,
):
    rock = lax.axis_index("rock")
    plane = lax.axis_index("plane")
    here = rock * TILES + plane
    nxt = lax.rem(here + 1, PARTS)
    prv = lax.rem(here + PARTS - 1, PARTS)
    next_part = (lax.div(nxt, TILES), lax.rem(nxt, TILES))
    prev_part = (lax.div(prv, TILES), lax.rem(prv, TILES))
    next_tile = (rock, lax.rem(plane + 1, TILES))
    prev_tile = (rock, lax.rem(plane + TILES - 1, TILES))

    def peer(o):
        return lax.rem(plane + o, TILES)

    barrier = pltpu.get_barrier_semaphore()
    for target in (next_part, prev_part):
        pl.semaphore_signal(barrier, inc=1, device_id=target, device_id_type=MESH)

    def greet(o, carry):
        pl.semaphore_signal(barrier, inc=1, device_id=(rock, peer(o)), device_id_type=MESH)
        return carry

    lax.fori_loop(1, TILES, greet, 0)

    def pair(outs, ins, index):
        return [
            pltpu.make_async_remote_copy(
                outs.at[0], ins.at[1], halo_send.at[index], halo_recv.at[index],
                device_id=prev_part, device_id_type=MESH),
            pltpu.make_async_remote_copy(
                outs.at[1], ins.at[0], halo_send.at[index + 1], halo_recv.at[index + 1],
                device_id=next_part, device_id_type=MESH),
        ]

    def edges(index):
        return [
            pltpu.make_async_remote_copy(
                edge_out.at[2 * index], edge_in.at[2 * index + 1], edge_send.at[2 * index],
                edge_recv.at[2 * index], device_id=prev_tile, device_id_type=MESH),
            pltpu.make_async_remote_copy(
                edge_out.at[2 * index + 1], edge_in.at[2 * index], edge_send.at[2 * index + 1],
                edge_recv.at[2 * index + 1], device_id=next_tile, device_id_type=MESH),
        ]

    def swap(outs, ins, sends, recvs, o):
        return pltpu.make_async_remote_copy(
            outs.at[peer(o)], ins.at[plane], sends.at[o - 1], recvs.at[o - 1],
            device_id=(rock, peer(o)), device_id_type=MESH)

    def start_all(*what):
        def one(o, carry):
            swap(*what, o).start()
            return carry
        lax.fori_loop(1, TILES, one, 0)
        outs, ins = what[:2]
        ins[plane] = outs[plane]

    def arrive_all(*what):
        def one(o, carry):
            swap(*what, o).wait_recv()
            return carry
        lax.fori_loop(1, TILES, one, 0)

    def sent_all(*what):
        def one(o, carry):
            swap(*what, o).wait_send()
            return carry
        lax.fori_loop(1, TILES, one, 0)

    tmap = tmap_ref[...]
    lift = lift_ref[...]
    th, tl = split(padded(tmap, QB))
    widen = ones_where(iota((Q, QB), 0) == iota((Q, QB), 1)).astype(BF16)
    tw[0:QB, :] = dot(th, widen).astype(BF16)
    tw[QB:2 * QB, :] = dot(tl, widen).astype(BF16)

    def put_state(x):
        high, rest = split(padded(x, QB))
        xh[0:QB, :] = high
        xl[0:QB, :] = rest

    def traces():
        first = dot(tw[...], xh[0:QB, :])
        return first[0:QP] + first[QB:QB + QP] + dot(tw[0:QB, :], xl[0:QB, :])[0:QP]

    def put_table(parts, start):
        rows = jnp.concatenate(
            [x[:, 256 * l:256 * l + 256] for x in parts for l in range(x.shape[1] // 256)], axis=0)
        high, rest = split(rows)
        table[start:start + rows.shape[0], 0:256] = high
        table[start:start + rows.shape[0], 256:512] = rest

    def pick(rows, which, count, height):
        got = rows[0:height]
        for l in range(1, count):
            got = jnp.where(which == l, rows[height * l:height * l + height], got)
        return got

    def fill_outgoing(out):
        for side in range(2):
            a = send_hot[:, HALO * side:HALO * side + HALO]
            rows = dot(table[0:320, :], jnp.concatenate([a, a], axis=0))
            out[side] = pick(rows, send_ref[side:side + 1, :] >> 8, 8, QP)

    def rims(rim):
        lower = jnp.where(here > 0, rim[0], 0.0)
        upper = jnp.where(here < PARTS - 1, rim[1], 0.0)
        return lower, upper

    face_of_row = lax.div(iota((QP, 1), 0), 9)

    def gather_faces(k):
        a = hot[:, ELEMS * k:ELEMS * k + ELEMS]
        rows = dot(table[...], jnp.concatenate([a, a], axis=0))
        got = pick(rows, nel_ref[k:k + 1, :] >> 8, 16, QP)
        got = jnp.where(face_of_row == nfa_ref[k:k + 1, :], got, 0.0)
        high, rest = split(padded(got, QB))
        xh[QB * (k + 1):QB * (k + 2), :] = high
        xl[QB * (k + 1):QB * (k + 2), :] = rest

    def change():
        first = dot(ww[...], xh[...])
        return first[0:QP] + first[QB:QB + QP] + dot(ww[0:QB, :], xl[...])[0:QP]

    s1[0:Q, :] = state_ref[...]
    s1[Q:QP, :] = jnp.zeros((QP - Q, ELEMS), F32)
    put_state(s1[...])
    tr = traces()
    put_table([tr], 0)

    def send_body(c, carry):
        for side in range(2):
            row = send_ref[side:side + 1, lanes(c)] & 255
            send_hot[:, lanes(8 * side + c)] = ones_where(iota((256, 128), 0) == row).astype(BF16)
        return carry

    lax.fori_loop(0, 8, send_body, 0, unroll=2)
    fill_outgoing(out1)
    pl.semaphore_wait(barrier, TILES + 1)
    for copy in pair(out1, rim1, 0):
        copy.start()
    edge_out[0] = press_ref[pl.ds(0, 64, stride=2), :]
    edge_out[1] = press_ref[pl.ds(1, 64, stride=2), :]
    for copy in edges(0):
        copy.start()

    tile = ftile_ref[...]
    upper = ones_where(iota((128, 128), 0) <= iota((128, 128), 1)).astype(BF16)
    count = jnp.concatenate([upper, jnp.ones((128, 128), BF16)], axis=0)
    before = ones_where(iota((64, 64), 1) < iota((64, 64), 0)).astype(BF16)
    named = [ones_where(tile == t).astype(BF16) for t in range(TILES)]
    earlier = dot(before, jnp.concatenate(named, axis=1)).astype(BF16)
    ranks = dot(
        jnp.concatenate(
            [jnp.concatenate([named[t], earlier[:, 128 * t:128 * t + 128]], axis=1) for t in range(TILES)],
            axis=0),
        count)
    place = jnp.zeros((64, 128), F32)
    for t in range(TILES):
        place = jnp.where(tile == t, ranks[64 * t:64 * t + 64] + (512.0 * t - 1.0), place)
    place = place.astype(I32)
    cell = fcell_ref[...]
    elem = fel_ref[...]
    slot = iota((64, 128), 0) * 128 + iota((64, 128), 1)
    live = jnp.where(slot < fcount_ref[0], 16, 0)
    slot_tab[0] = place >> 7
    slot_tab[1] = place & 127
    slot_tab[2] = ((cell >> 7) & 63) * 2 + (cell >> 13)
    slot_tab[3] = cell & 127
    slot_tab[4] = elem & 127
    slot_tab[5] = (elem >> 7) + live

    def order_body(c, carry):
        at = pl.ds(c, 1)
        mine = iota((64, 128), 0) == slot_tab[0, at, :]
        for v in range(4):
            va[64 * v:64 * v + 64, lanes(c)] = jnp.where(mine, slot_tab[2 + v, at, :], 0).astype(F32).astype(BF16)
        vb[0:128, lanes(c)] = ones_where(iota((128, 128), 0) == slot_tab[1, at, :]).astype(BF16)
        return carry

    lax.fori_loop(0, 64, order_body, 0, unroll=2)
    grouped = dot_nt(va[...], vb[0:128, :])
    code = grouped[0:64] * 128.0 + grouped[64:128]
    for t in range(TILES):
        cells_out[t] = code[4 * t:4 * t + 4]
    elem_row[0] = grouped[128:192]
    elem_row[1] = grouped[192:256]
    start_all(cells_out, cells_in, cell_send, cell_recv)

    def elem_body(c, carry):
        row = elem_row[0, pl.ds(c, 1), :]
        elem_hot[:, lanes(c)] = ones_where(iota((128, 128), 0).astype(F32) == row).astype(BF16)
        return carry

    lax.fori_loop(0, 64, elem_body, 0, unroll=2)

    for k in range(4):
        def hot_body(c, carry):
            row = nel_ref[k:k + 1, lanes(c)] & 255
            hot[:, lanes(16 * k + c)] = ones_where(iota((256, 128), 0) == row).astype(BF16)
            return carry

        lax.fori_loop(0, 16, hot_body, 0, unroll=2)

    row_i = iota((Q, 256), 0)
    col_i = iota((Q, 256), 1)
    own_block = ones_where(row_i == col_i).astype(BF16)
    blk = lax.div(col_i, QB)
    inner = lax.rem(col_i, QB)
    face_block = ones_where(
        (blk >= 1) & (blk <= 4) & (inner < Q) & (row_i == 9 * (blk - 1) + lax.rem(inner, 9))).astype(BF16)
    volume = stiff_ref[...] - exact_dot(lift, tmap)
    mh, ml = split(padded(volume, QB))
    lh, ll = split(padded(lift, QB))
    ww[0:QB, :] = (dot(mh, own_block) + dot(lh, face_block)).astype(BF16)
    ww[QB:2 * QB, :] = (dot(ml, own_block) + dot(ll, face_block)).astype(BF16)
    xh[5 * QB:256, :] = jnp.zeros((16, ELEMS), BF16)
    xl[5 * QB:256, :] = jnp.zeros((16, ELEMS), BF16)

    push = column(tdir_ref[...])
    tau = exact_dot(tmap, push[0:Q])
    same = ones_where(lax.rem(iota((Q, Q), 0), 9) == lax.rem(iota((Q, Q), 1), 9))
    of_facet = jnp.where(lax.div(iota((Q, 128), 0), 9) == lax.rem(iota((Q, 128), 1), 4), tau, 0.0)
    spread = jnp.where(
        lax.div(iota((Q, 128), 0), 9) == lax.div(iota((Q, 128), 1), 4), exact_dot(same, of_facet), 0.0)
    load_map = jnp.where(
        iota((Q, 128), 1) == 16, exact_dot(volume, push[0:Q]), exact_dot(lift, spread))
    uh, ul = split(padded(load_map, QB))
    uu[0:QB, :] = uh
    uu[QB:2 * QB, :] = ul

    for copy in pair(out1, rim1, 0):
        copy.wait_recv()
    put_table(list(rims(rim1)), 320)
    for k in range(4):
        gather_faces(k)
    scale = STEP * jac_ref[...]
    s1[...] = s1[...] + scale * change()

    score = jnp.sum(column(odir_ref[...]) * s1[...], axis=0, keepdims=True)
    opening = 0.2 * (jnp.maximum(score, 0.0) + jnp.log1p(jnp.exp(-jnp.abs(score))))
    oh, ol = split(jnp.concatenate([opening[:, 128 * i:128 * i + 128] for i in range(16)], axis=0))
    got = dot(jnp.concatenate([oh, ol], axis=0), elem_hot[...])
    val[0:16, :] = got[0:16] + got[16:32]
    sixteen = (iota((16, 128), 0) + 16).astype(F32)

    def open_body(t, carry):
        for r in range(4):
            mine = sixteen == elem_row[1, pl.ds(4 * t + r, 1), :]
            open_out[t, r:r + 1, :] = jnp.sum(
                jnp.where(mine, val[0:16, lanes(4 * t + r)], 0.0), axis=0, keepdims=True)
        return carry

    lax.fori_loop(0, TILES, open_body, 0, unroll=2)
    start_all(open_out, open_in, open_send, open_recv)

    put_state(s1[...])
    tr = traces()
    put_table([tr], 0)
    fill_outgoing(out2)
    for copy in pair(out2, rim2, 2):
        copy.start()

    arrive_all(cells_out, cells_in, cell_send, cell_recv)

    def cell_body(t, carry):
        for r in range(4):
            c = 4 * t + r
            at = cells_in[t, r:r + 1, :].astype(I32)
            cell_hi[:, lanes(c)] = ones_where(iota((128, 128), 0) == (at >> 7)).astype(BF16)
            cell_lo[:, lanes(c)] = ones_where(iota((128, 128), 0) == (at & 127)).astype(BF16)
        return carry

    lax.fori_loop(0, TILES, cell_body, 0)
    arrive_all(open_out, open_in, open_send, open_recv)

    def amount_body(t, carry):
        for r in range(4):
            c = 4 * t + r
            high, rest = split(jnp.broadcast_to(open_in[t, r:r + 1, :], (128, 128)))
            unit = cell_lo[:, lanes(c)]
            vb[0:128, lanes(c)] = unit * high
            vb[128:256, lanes(c)] = unit * rest
        return carry

    lax.fori_loop(0, TILES, amount_body, 0)
    field = dot_nt(cell_hi[...], vb[...])
    aper = base_ref[...] + (field[:, 0:128] + field[:, 128:256])
    aper_ref[...] = aper
    c = aper * aper * aper / 12.0
    cond[...] = c
    edge_out[2] = cond[pl.ds(0, 64, stride=2), :]
    edge_out[3] = cond[pl.ds(1, 64, stride=2), :]
    for copy in edges(1):
        copy.start()

    for copy in pair(out2, rim2, 2):
        copy.wait_recv()
    put_table(list(rims(rim2)), 320)
    gather_faces(0)

    p = press_ref[...]
    odd = (iota((128, 128), 0) & 1) == 1
    lane = iota((128, 128), 1)
    block = iota((128, 128), 0) >> 1
    for copy in edges(0) + edges(1):
        copy.wait_recv()
    for i in range(2):
        edge_wide[i, pl.ds(0, 64, stride=2), :] = edge_in[2 * i]
        edge_wide[i, pl.ds(1, 64, stride=2), :] = edge_in[2 * i + 1]

    def sides(x, wide):
        after = pltpu.roll(x, 127, 1)
        after = jnp.where(lane == 127, pltpu.roll(after, 126, 0), after)
        ahead = pltpu.roll(x, 1, 1)
        ahead = jnp.where(lane == 0, pltpu.roll(ahead, 2, 0), ahead)
        up = jnp.where(odd, pltpu.roll(x, 1, 0), wide)
        down = jnp.where(odd, wide, pltpu.roll(x, 127, 0))
        inside = (
            (lane < 127) | (block < 63),
            (lane > 0) | (block > 0),
            odd | (plane > 0),
            jnp.logical_not(odd) | (plane < TILES - 1),
        )
        return [jnp.where(m, v, 0.0) for m, v in zip(inside, (after, ahead, up, down))]

    inflow = jnp.zeros((128, 128), F32)
    for other_p, other_c in zip(sides(p, edge_wide[0]), sides(c, edge_wide[1])):
        inflow = inflow + 2.0 * c * other_c / (c + other_c) * (other_p - p)
    new_p = p + RATE * (inflow + inj_ref[...])
    new_press_ref[...] = new_p

    ph, prest = split(new_p)
    units = cell_lo[...]
    val[...] = dot(jnp.concatenate([ph, prest], axis=1), jnp.concatenate([units, units], axis=0))

    def press_body(t, carry):
        for r in range(4):
            mine = iota((128, 128), 0) == (cells_in[t, r:r + 1, :].astype(I32) >> 7)
            press_out[t, r:r + 1, :] = jnp.sum(
                jnp.where(mine, val[:, lanes(4 * t + r)], 0.0), axis=0, keepdims=True)
        return carry

    lax.fori_loop(0, TILES, press_body, 0)
    start_all(press_out, press_in, pr_send, pr_recv)
    gather_faces(1)
    gather_faces(2)
    arrive_all(press_out, press_in, pr_send, pr_recv)

    def load_body(t, carry):
        for r in range(4):
            c = 4 * t + r
            mine = sixteen == elem_row[1, pl.ds(c, 1), :]
            high, rest = split(jnp.where(mine, press_in[t, r:r + 1, :], 0.0))
            va[0:16, lanes(c)] = high
            va[16:32, lanes(c)] = rest
        return carry

    lax.fori_loop(0, TILES, load_body, 0, unroll=2)
    load = dot_nt(va[0:32, :], elem_hot[...])
    load = load[0:16] + load[16:32]
    for i in range(16):
        lane_row[:, 128 * i:128 * i + 128] = load[i:i + 1]
    w = scale * lane_row[...]
    own_w = jnp.concatenate([w[:, 256 * l:256 * l + 256] for l in range(8)], axis=0)
    wh, wl = split(own_w)
    got = dot(jnp.concatenate([wh, wl], axis=0), send_hot[...])
    got = got[0:8] + got[8:16]
    for side in range(2):
        mine = iota((8, HALO), 0) == (send_ref[side:side + 1, :] >> 8)
        wout[side] = jnp.sum(
            jnp.where(mine, got[:, HALO * side:HALO * side + HALO], 0.0), axis=0, keepdims=True)
    for copy in pair(wout, wrim, 4):
        copy.start()
    gather_faces(3)
    change1[...] = change()
    for copy in pair(wout, wrim, 4):
        copy.wait_recv()
    low, high_rim = rims(wrim)
    far_w = jnp.concatenate([x[:, 256 * l:256 * l + 256] for x in (low, high_rim) for l in range(4)], axis=0)
    wh, wl = split(jnp.concatenate([own_w, far_w], axis=0))
    got = dot(jnp.concatenate([wh, wl], axis=0), hot[...])
    got = got[0:16] + got[16:32]
    near = []
    for k in range(4):
        mine = iota((16, ELEMS), 0) == (nel_ref[k:k + 1, :] >> 8)
        near_w = jnp.sum(jnp.where(mine, got[:, ELEMS * k:ELEMS * k + ELEMS], 0.0), axis=0, keepdims=True)
        near.append(jnp.where(iota((4, ELEMS), 0) == nfa_ref[k:k + 1, :], near_w, 0.0))
    near.append(w)
    near.append(jnp.zeros((128 - 17, ELEMS), F32))
    nh, nl = split(jnp.concatenate(near, axis=0))
    first = dot(uu[...], nh)
    extra = first[0:QP] + first[QB:QB + QP] + dot(uu[0:QB, :], nl)[0:QP]
    result = s1[...] + push * w + scale * (change1[...] + extra)
    new_state_ref[...] = result[0:Q]

    for index, (outs, ins) in enumerate(((out1, rim1), (out2, rim2), (wout, wrim))):
        for copy in pair(outs, ins, 2 * index):
            copy.wait_send()
    for copy in edges(0) + edges(1):
        copy.wait_send()
    sent_all(cells_out, cells_in, cell_send, cell_recv)
    sent_all(open_out, open_in, open_send, open_recv)
    sent_all(press_out, press_in, pr_send, pr_recv)


def interleaved(x):
    return x.reshape(2, 64, 128).transpose(1, 0, 2).reshape(128, 128)


def straight(x):
    return x.reshape(64, 2, 128).transpose(1, 0, 2).reshape(1, 2, 8192)


def shards(
    rock_state, jacobian, stiffness, trace_map, lift_map, neighbor_elem, neighbor_face, send_elem,
    opening_dir, traction_dir, face_elem, face_tile, face_cell, face_count, pressure, base_aperture, injection,
):
    vmem = pl.BlockSpec(memory_space=pltpu.VMEM)
    smem = pl.BlockSpec(memory_space=pltpu.SMEM)
    scratch = [
        pltpu.VMEM((QP, ELEMS), F32),
        pltpu.VMEM((640, 512), BF16),
        pltpu.VMEM((256, SLOTS), BF16),
        pltpu.VMEM((256, 2 * HALO), BF16),
        pltpu.VMEM((256, ELEMS), BF16),
        pltpu.VMEM((256, ELEMS), BF16),
        pltpu.VMEM((2 * QB, 256), BF16),
        pltpu.VMEM((2 * QB, QB), BF16),
        pltpu.VMEM((2 * QB, 128), BF16),
        pltpu.VMEM((2, QP, HALO), F32),
        pltpu.VMEM((2, QP, HALO), F32),
        pltpu.VMEM((2, QP, HALO), F32),
        pltpu.VMEM((2, QP, HALO), F32),
        pltpu.VMEM((2, 1, HALO), F32),
        pltpu.VMEM((2, 1, HALO), F32),
        pltpu.VMEM((256, SLOTS), BF16),
        pltpu.VMEM((256, SLOTS), BF16),
        pltpu.VMEM((128, SLOTS), BF16),
        pltpu.VMEM((2, 64, 128), F32),
        pltpu.VMEM((TILES, 4, 128), F32),
        pltpu.VMEM((TILES, 4, 128), F32),
        pltpu.VMEM((TILES, 4, 128), F32),
        pltpu.VMEM((TILES, 4, 128), F32),
        pltpu.VMEM((TILES, 4, 128), F32),
        pltpu.VMEM((TILES, 4, 128), F32),
        pltpu.VMEM((6, 64, 128), I32),
        pltpu.VMEM((128, SLOTS), BF16),
        pltpu.VMEM((128, SLOTS), BF16),
        pltpu.VMEM((128, SLOTS), F32),
        pltpu.VMEM((128, 128), F32),
        pltpu.VMEM((4, 64, 128), F32),
        pltpu.VMEM((4, 64, 128), F32),
        pltpu.VMEM((2, 128, 128), F32),
        pltpu.VMEM((QP, ELEMS), F32),
        pltpu.VMEM((1, ELEMS), F32),
    ] + [pltpu.SemaphoreType.DMA((n,)) for n in (6, 6, 15, 15, 15, 15, 15, 15, 4, 4)]
    new_state, new_pressure, aperture = pl.pallas_call(
        kernel,
        out_shape=(
            jax.ShapeDtypeStruct((Q, ELEMS), F32),
            jax.ShapeDtypeStruct((128, 128), F32),
            jax.ShapeDtypeStruct((128, 128), F32),
        ),
        in_specs=[vmem] * 13 + [smem] + [vmem] * 3,
        out_specs=(vmem,) * 3,
        scratch_shapes=scratch,
        compiler_params=pltpu.CompilerParams(
            collective_id=0, has_side_effects=True, vmem_limit_bytes=56 * 2**20),
    )(
        rock_state, jacobian.reshape(1, ELEMS), stiffness, trace_map, lift_map, neighbor_elem, neighbor_face,
        send_elem, opening_dir.reshape(1, Q), traction_dir.reshape(1, Q), face_elem.reshape(64, 128),
        face_tile.reshape(64, 128), face_cell.reshape(64, 128), face_count, interleaved(pressure),
        interleaved(base_aperture), interleaved(injection),
    )
    return new_state, straight(new_pressure), straight(aperture)


def solution(mesh):
    elems = P(None, ("rock", "plane"))
    flat = P(("rock", "plane"))
    grid = P("rock", "plane", None)
    return jax.shard_map(
        shards,
        mesh=mesh,
        in_specs=(elems, flat, P(), P(), P(), elems, elems, elems, P(), P(), flat, flat, flat, flat, grid, grid, grid),
        out_specs=(elems, grid, grid),
        check_vma=False,
    )
```

time: 518 us -> 58.7 us (0.11); the launches traced: 512 us -> 58.5 us
  local copies, waits for them, and re-layouts: 235 us -> 3.25 us
  waiting for transfers between devices: 141 us -> 0 us
  other arithmetic: 90.6 us -> 0 us
  Pallas kernels: 0 us -> 54 us
  starting transfers between devices: 24 us -> 0 us
  between operations: 15.9 us -> 1.3 us
    gather x12 -> x0, local copies, waits for them, and re-layouts: 216 us -> none  [the longest x1 96.4 us: shards(): face_pressure = whole[grid_cell]]
    unnamed x3 -> x0, waiting for transfers between devices: 87.9 us -> none
    scatter-add x2 -> x0, other arithmetic: 87.7 us -> none  [the longest x1 44.2 us: shards(): jnp.zeros((tiles * tile_cells,), jnp.float32).at[grid_cell].add(openings)]
    pallas_call x0 -> x1, Pallas kernels: none -> 54 us  [shards(): pl.pallas_call(kernel, out_shape=(jax.ShapeDtypeStruct((Q, ELEMS), F32),...]
    all_gather x1 -> x0, waiting for transfers between devices: 47.1 us -> none  [shards(): lax.all_gather(new_pressure.reshape(-1), 'plane', axis=0, tiled=True)]
    ppermute x6 -> x0, starting transfers between devices: 24 us -> none  [the longest x3 14.3 us: extended_2(): lax.ppermute(lax.slice_in_dim(block, 0, width, axis=dim), axis, backward)]
    transpose x2 -> x0, local copies, waits for them, and re-layouts: 9.39 us -> none  [neighbor_jumps(): folded = trace_pool.reshape(4, width, pool_columns).transpose(1, 0, 2).re...]
    ppermute x6 -> x0, waiting for transfers between devices: 6.3 us -> none  [the longest x3 5.98 us: extended_2(): lax.ppermute(lax.slice_in_dim(block, 0, width, axis=dim), axis, backward)]
  transfers between devices with their start and end apart: 8 -> 0, of which waited for: 6 -> 0; matrix products, arithmetic and copies ran while one was open for 1% -> 0% of each run, Pallas kernels for 0% -> 0%
where the time goes in v1:
time: 58.7 us; the launch traced here: 58.5 us
  Pallas kernels  54 us (92%)
  local copies, waits for them, and re-layouts  3.25 us (6%)
  between operations  1.3 us (2%)
    pallas_call x1, Pallas kernels, shards(): pl.pallas_call(kernel, out_shape=(jax.ShapeDtypeStruct((Q, ELEMS), F32),...  54 us
    unnamed x7, local copies, waits for them, and re-layouts  3.25 us

profile of v1, /device:TPU:1, one launch (start us, length us, event | category | flops | bytes accessed | tf_op | source)
XLA Modules:
  0.0 58.5 jit_solution(6702790080246219796)
XLA Ops:
  1.3 54.0 %shard_map.184 = (f32[36,2048]{1,0:T(8,128)}, f32[128,128]{1,0:T(8,128)}, f32[128,128]{1,0:T(8,128)}) custom-call(f32[36,2048]{1,0:T(8,128)} %state_ref.1, f32[1,2048]{1,0:T(1,128)} %bitcast.39, f32[36,36]{1,0:T(8,128)} %stiff_ref.1, f32[36,36]{1,0:T(8,128)} %tmap_ref.1, f32[36,36]{1,0:T(8,128)} %lift_ref.1, s32[4,2048]{1,0:T(4,128)} %nel_ref.1, ...), custom_call_target="tpu_custom_call" | custom-call | tf_op jit(solution)/shard_map/pallas_call | solution.py:528
  55.2 0.0 copy-start.1
  55.3 1.8 %copy.29 = f32[36,2048]{1,0:T(8,128)} copy(f32[36,2048]{1,0:T(8,128)} %get-tuple-element.12) | data formatting | bytes 589824
  57.0 0.0 copy-done.1
  57.0 0.0 copy-start
  57.0 0.6 %copy.30 = f32[1,2,8192]{2,1,0:T(2,128)} copy(f32[1,2,8192]{2,1,0:T(2,128)S(1)} %bitcast.32) | data formatting | bytes 131072
  57.6 0.2 copy-done
  57.9 0.6 %copy.31 = f32[1,2,8192]{2,1,0:T(2,128)} copy(f32[1,2,8192]{2,1,0:T(2,128)S(1)} %bitcast.31) | data formatting | bytes 131072
Async XLA Ops:
  55.2 1.8 %copy-start.1 = (f32[128,128]{1,0:T(8,128)S(1)}, f32[128,128]{1,0:T(8,128)}, u32[]{:S(2)}) copy-start(f32[128,128]{1,0:T(8,128)} %get-tuple-element.7) | copy-start | bytes 196612
  57.0 0.9 %copy-start = (f32[128,128]{1,0:T(8,128)S(1)}, f32[128,128]{1,0:T(8,128)}, u32[]{:S(2)}) copy-start(f32[128,128]{1,0:T(8,128)} %get-tuple-element.8) | copy-start | bytes 196612

commit v2 on v1

--- a/solution.py
+++ b/solution.py
@@ -46,6 +46,10 @@
     return jnp.where(mask, 1.0, 0.0).astype(F32)
 
 
+def units(count, row):
+    return ones_where(iota((count, row.shape[1]), 0) == row).astype(BF16)
+
+
 def lanes(chunk, width=128):
     return pl.ds(pl.multiple_of(chunk * width, width), width)
 
@@ -61,14 +65,26 @@
 
 
 def kernel(
+    state_hbm, jac_hbm, stiff_hbm, tmap_hbm, lift_hbm, nel_hbm, nfa_hbm, send_hbm, odir_hbm, tdir_hbm,
+    fel_hbm, ftile_hbm, fcell_hbm, fcount_ref, press_hbm, base_hbm, inj_hbm,
+    new_state_ref, new_press_ref, aper_ref,
+    s1, table, hot, send_hot, xh, xl, ww, tw, uu, gw, gtab, out1, out2, rim1, rim2, wout, wrim,
+    elem_hot, elem_hi, elem_lo, cells_out, cells_in, open_out, open_in, press_out, press_in,
+    slot_tab, cell_hot, cell_unit, cell_row, cond, edge_out, edge_in, edge_wide, own2, lane_row, slot_row,
     state_ref, jac_ref, stiff_ref, tmap_ref, lift_ref, nel_ref, nfa_ref, send_ref, odir_ref, tdir_ref,
-    fel_ref, ftile_ref, fcell_ref, fcount_ref, press_ref, base_ref, inj_ref,
-    new_state_ref, new_press_ref, aper_ref,
-    s1, table, hot, send_hot, xh, xl, ww, tw, uu, out1, out2, rim1, rim2, wout, wrim,
-    va, vb, elem_hot, elem_row, cells_out, cells_in, open_out, open_in, press_out, press_in,
-    slot_tab, cell_hi, cell_lo, val, cond, edge_out, edge_in, edge_wide, change1, lane_row,
+    fel_ref, ftile_ref, fcell_ref, press_ref, base_ref, inj_ref, in_sem,
     halo_send, halo_recv, cell_send, cell_recv, open_send, open_recv, pr_send, pr_recv, edge_send, edge_recv,
 ):
+    loads = [
+        pltpu.make_async_copy(source, target, in_sem.at[i])
+        for i, (source, target) in enumerate((
+            (state_hbm, state_ref), (tmap_hbm, tmap_ref), (send_hbm, send_ref), (lift_hbm, lift_ref),
+            (ftile_hbm, ftile_ref), (fcell_hbm, fcell_ref), (fel_hbm, fel_ref), (press_hbm, press_ref),
+            (nel_hbm, nel_ref), (nfa_hbm, nfa_ref), (stiff_hbm, stiff_ref), (odir_hbm, odir_ref),
+            (jac_hbm, jac_ref), (tdir_hbm, tdir_ref), (base_hbm, base_ref), (inj_hbm, inj_ref)))
+    ]
+    for load in loads[:4]:
+        load.start()
     rock = lax.axis_index("rock")
     plane = lax.axis_index("plane")
     here = rock * TILES + plane
@@ -91,6 +107,8 @@
         return carry
 
     lax.fori_loop(1, TILES, greet, 0)
+    for load in loads[4:]:
+        load.start()
 
     def pair(outs, ins, index):
         return [
@@ -137,10 +155,12 @@
             return carry
         lax.fori_loop(1, TILES, one, 0)
 
+    for load in loads[:4]:
+        load.wait()
     tmap = tmap_ref[...]
     lift = lift_ref[...]
+    widen = ones_where(iota((Q, QB), 0) == iota((Q, QB), 1)).astype(BF16)
     th, tl = split(padded(tmap, QB))
-    widen = ones_where(iota((Q, QB), 0) == iota((Q, QB), 1)).astype(BF16)
     tw[0:QB, :] = dot(th, widen).astype(BF16)
     tw[QB:2 * QB, :] = dot(tl, widen).astype(BF16)
 
@@ -160,17 +180,17 @@
         table[start:start + rows.shape[0], 0:256] = high
         table[start:start + rows.shape[0], 256:512] = rest
 
-    def pick(rows, which, count, height):
-        got = rows[0:height]
-        for l in range(1, count):
-            got = jnp.where(which == l, rows[height * l:height * l + height], got)
+    def pick(got, rows, which, first, count):
+        for l in range(count):
+            part = rows[QP * l:QP * l + QP]
+            got = part if got is None else jnp.where(which == first + l, part, got)
         return got
 
     def fill_outgoing(out):
         for side in range(2):
             a = send_hot[:, HALO * side:HALO * side + HALO]
             rows = dot(table[0:320, :], jnp.concatenate([a, a], axis=0))
-            out[side] = pick(rows, send_ref[side:side + 1, :] >> 8, 8, QP)
+            out[side] = pick(None, rows, send_ref[side:side + 1, :] >> 8, 0, 8)
 
     def rims(rim):
         lower = jnp.where(here > 0, rim[0], 0.0)
@@ -179,14 +199,24 @@
 
     face_of_row = lax.div(iota((QP, 1), 0), 9)
 
-    def gather_faces(k):
+    def columns(k, rows):
         a = hot[:, ELEMS * k:ELEMS * k + ELEMS]
-        rows = dot(table[...], jnp.concatenate([a, a], axis=0))
-        got = pick(rows, nel_ref[k:k + 1, :] >> 8, 16, QP)
+        return dot(rows, jnp.concatenate([a, a], axis=0))
+
+    def put_faces(k, got):
         got = jnp.where(face_of_row == nfa_ref[k:k + 1, :], got, 0.0)
         high, rest = split(padded(got, QB))
         xh[QB * (k + 1):QB * (k + 2), :] = high
         xl[QB * (k + 1):QB * (k + 2), :] = rest
+
+    def gather_faces(k):
+        put_faces(k, pick(None, columns(k, table[...]), nel_ref[k:k + 1, :] >> 8, 0, 16))
+
+    def gather_own(k):
+        own2[k] = pick(None, columns(k, table[0:320, :]), nel_ref[k:k + 1, :] >> 8, 0, 8)
+
+    def gather_rims(k):
+        put_faces(k, pick(own2[k], columns(k, table[320:640, :]), nel_ref[k:k + 1, :] >> 8, 8, 8))
 
     def change():
         first = dot(ww[...], xh[...])
@@ -198,17 +228,14 @@
     tr = traces()
     put_table([tr], 0)
 
-    def send_body(c, carry):
-        for side in range(2):
-            row = send_ref[side:side + 1, lanes(c)] & 255
-            send_hot[:, lanes(8 * side + c)] = ones_where(iota((256, 128), 0) == row).astype(BF16)
-        return carry
-
-    lax.fori_loop(0, 8, send_body, 0, unroll=2)
+    for side in range(2):
+        send_hot[:, HALO * side:HALO * side + HALO] = units(256, send_ref[side:side + 1, :] & 255)
     fill_outgoing(out1)
     pl.semaphore_wait(barrier, TILES + 1)
     for copy in pair(out1, rim1, 0):
         copy.start()
+    for load in loads[4:]:
+        load.wait()
     edge_out[0] = press_ref[pl.ds(0, 64, stride=2), :]
     edge_out[1] = press_ref[pl.ds(1, 64, stride=2), :]
     for copy in edges(0):
@@ -231,46 +258,105 @@
     place = place.astype(I32)
     cell = fcell_ref[...]
     elem = fel_ref[...]
+    row = ((cell >> 7) & 63) * 2 + (cell >> 13)
+    code = (row & 63) * 256 + (row >> 6) * 128 + (cell & 127)
     slot = iota((64, 128), 0) * 128 + iota((64, 128), 1)
-    live = jnp.where(slot < fcount_ref[0], 16, 0)
-    slot_tab[0] = place >> 7
-    slot_tab[1] = place & 127
-    slot_tab[2] = ((cell >> 7) & 63) * 2 + (cell >> 13)
-    slot_tab[3] = cell & 127
-    slot_tab[4] = elem & 127
-    slot_tab[5] = (elem >> 7) + live
-
-    def order_body(c, carry):
-        at = pl.ds(c, 1)
-        mine = iota((64, 128), 0) == slot_tab[0, at, :]
-        for v in range(4):
-            va[64 * v:64 * v + 64, lanes(c)] = jnp.where(mine, slot_tab[2 + v, at, :], 0).astype(F32).astype(BF16)
-        vb[0:128, lanes(c)] = ones_where(iota((128, 128), 0) == slot_tab[1, at, :]).astype(BF16)
-        return carry
-
-    lax.fori_loop(0, 64, order_body, 0, unroll=2)
-    grouped = dot_nt(va[...], vb[0:128, :])
-    code = grouped[0:64] * 128.0 + grouped[64:128]
+    live = jnp.where(slot < fcount_ref[0], 128, 0)
+    slot_tab[0] = (place >> 7).astype(F32)
+    slot_tab[1] = (place & 127).astype(F32)
+    slot_tab[2] = ((code >> 5) - 256).astype(F32)
+    slot_tab[3] = ((code & 31) * 16 + (elem >> 7) - 256).astype(F32)
+    slot_tab[4] = ((elem & 127) + live).astype(F32)
+
+    row64 = iota((64, 128), 0).astype(F32)
+    row128 = iota((128, 128), 0).astype(F32)
+
+    def order_body(half, total):
+        named = []
+        inner = []
+        for u in range(32):
+            at = pl.ds(32 * half + u, 1)
+            mine = row64 == slot_tab[0, at, :]
+            named.append(jnp.concatenate(
+                [jnp.where(mine, slot_tab[2 + v, at, :], 0.0).astype(BF16) for v in range(3)], axis=0))
+            inner.append(ones_where(row128 == slot_tab[1, at, :]).astype(BF16))
+        return total + dot_nt(jnp.concatenate(named, axis=1), jnp.concatenate(inner, axis=1))
+
+    grouped = lax.fori_loop(0, 2, order_body, jnp.zeros((192, 128), F32)).astype(I32)
+    middle = grouped[64:128] + 256
+    code = ((grouped[0:64] + 256) * 32 + (middle >> 4)).astype(F32)
+    high = ((middle & 15) + ((grouped[128:192] >> 7) << 4)).astype(F32)
+    low = (grouped[128:192] & 127).astype(F32)
+    for c in range(64):
+        at = slice(128 * c, 128 * c + 128)
+        inner = slice(128 * (c % 4), 128 * (c % 4) + 128)
+        cells_out[c // 4, :, inner] = code[c:c + 1]
+        elem_hi[:, at] = high[c:c + 1]
+        elem_lo[:, at] = low[c:c + 1]
+    start_all(cells_out, cells_in, cell_send, cell_recv)
+
+    for k in range(4):
+        hot[:, ELEMS * k:ELEMS * k + ELEMS] = units(256, nel_ref[k:k + 1, :] & 255)
+
+    for k in range(4):
+        at = slice(2048 * k, 2048 * k + 2048)
+        elem_hot[:, at] = units(128, elem_lo[:, at].astype(I32))
+
+    volume = stiff_ref[...] - exact_dot(lift, tmap)
+    same = ones_where(lax.rem(iota((Q, Q), 0), 9) == lax.rem(iota((Q, Q), 1), 9))
+    odir = odir_ref[...]
+    of_face = jnp.where(lax.div(iota((16, Q), 0), 4) == lax.div(iota((16, Q), 1), 9), exact_dot(odir, lift), 0.0)
+    of_face = exact_dot(of_face, same)
+    gh, gl = split(jnp.where(lax.rem(iota((16, Q), 0), 4) == lax.div(iota((16, Q), 1), 9), of_face, 0.0))
+    gw[0:16, :] = dot(gh, widen).astype(BF16)
+    gw[16:32, :] = dot(gl, widen).astype(BF16)
+
+    def put_scores(parts, start):
+        for x in parts:
+            high, rest = split(padded(x, QB))
+            got = dot(gw[...], high)
+            got = got[0:16] + got[16:32] + dot(gw[0:16, :], rest)
+            for l in range(x.shape[1] // 256):
+                for half in range(2):
+                    at = 256 * l + 128 * half
+                    gtab[half, pl.ds(start + l, 16, stride=16), :] = got[:, at:at + 128]
+            start += x.shape[1] // 256
+
+    put_scores([tr], 0)
+    scale = STEP * jac_ref[...]
+    own_state = s1[...]
+    direct = jnp.sum(column(odir) * own_state, axis=0, keepdims=True)
+    within = jnp.sum(column(exact_dot(odir, volume)) * own_state, axis=0, keepdims=True)
+
+    for copy in pair(out1, rim1, 0):
+        copy.wait_recv()
+    put_scores(rims(rim1), 8)
+    for k in range(4):
+        at = slice(64 * k, 64 * k + 64)
+        gh, gl = split(jnp.concatenate([gtab[0, at, :], gtab[1, at, :]], axis=1))
+        got = dot(jnp.concatenate([gh, gl], axis=0), hot[:, ELEMS * k:ELEMS * k + ELEMS])
+        mine = iota((64, ELEMS), 0) == nfa_ref[k:k + 1, :] * 16 + (nel_ref[k:k + 1, :] >> 8)
+        within = within + jnp.sum(jnp.where(mine, got[0:64] + got[64:128], 0.0), axis=0, keepdims=True)
+    score = direct + scale * within
+
+    opening = 0.2 * (jnp.maximum(score, 0.0) + jnp.log1p(jnp.exp(-jnp.abs(score))))
+    oh, ol = split(jnp.concatenate([opening[:, 128 * i:128 * i + 128] for i in range(16)], axis=0))
+    got = dot(jnp.concatenate([oh, ol], axis=0), elem_hot[...])
+    sixteen = (iota((16, 1), 0) + 16).astype(F32)
+    picked = jnp.sum(
+        jnp.where(sixteen == elem_hi[...], got[0:16] + got[16:32], 0.0), axis=0, keepdims=True)
     for t in range(TILES):
-        cells_out[t] = code[4 * t:4 * t + 4]
-    elem_row[0] = grouped[128:192]
-    elem_row[1] = grouped[192:256]
-    start_all(cells_out, cells_in, cell_send, cell_recv)
-
-    def elem_body(c, carry):
-        row = elem_row[0, pl.ds(c, 1), :]
-        elem_hot[:, lanes(c)] = ones_where(iota((128, 128), 0).astype(F32) == row).astype(BF16)
-        return carry
-
-    lax.fori_loop(0, 64, elem_body, 0, unroll=2)
-
-    for k in range(4):
-        def hot_body(c, carry):
-            row = nel_ref[k:k + 1, lanes(c)] & 255
-            hot[:, lanes(16 * k + c)] = ones_where(iota((256, 128), 0) == row).astype(BF16)
-            return carry
-
-        lax.fori_loop(0, 16, hot_body, 0, unroll=2)
+        open_out[t] = picked[:, 512 * t:512 * t + 512]
+    start_all(open_out, open_in, open_send, open_recv)
+
+    arrive_all(cells_out, cells_in, cell_send, cell_recv)
+
+    for t in range(TILES):
+        at = slice(512 * t, 512 * t + 512)
+        where = cells_in[t].astype(I32)
+        cell_hot[:, at] = units(256, where & 255)
+        cell_unit[:, at] = units(64, where >> 8)
+        cell_row[:, at] = where >> 8
 
     row_i = iota((Q, 256), 0)
     col_i = iota((Q, 256), 1)
@@ -279,83 +365,28 @@
     inner = lax.rem(col_i, QB)
     face_block = ones_where(
         (blk >= 1) & (blk <= 4) & (inner < Q) & (row_i == 9 * (blk - 1) + lax.rem(inner, 9))).astype(BF16)
-    volume = stiff_ref[...] - exact_dot(lift, tmap)
     mh, ml = split(padded(volume, QB))
     lh, ll = split(padded(lift, QB))
     ww[0:QB, :] = (dot(mh, own_block) + dot(lh, face_block)).astype(BF16)
     ww[QB:2 * QB, :] = (dot(ml, own_block) + dot(ll, face_block)).astype(BF16)
     xh[5 * QB:256, :] = jnp.zeros((16, ELEMS), BF16)
     xl[5 * QB:256, :] = jnp.zeros((16, ELEMS), BF16)
-
-    push = column(tdir_ref[...])
-    tau = exact_dot(tmap, push[0:Q])
-    same = ones_where(lax.rem(iota((Q, Q), 0), 9) == lax.rem(iota((Q, Q), 1), 9))
-    of_facet = jnp.where(lax.div(iota((Q, 128), 0), 9) == lax.rem(iota((Q, 128), 1), 4), tau, 0.0)
-    spread = jnp.where(
-        lax.div(iota((Q, 128), 0), 9) == lax.div(iota((Q, 128), 1), 4), exact_dot(same, of_facet), 0.0)
-    load_map = jnp.where(
-        iota((Q, 128), 1) == 16, exact_dot(volume, push[0:Q]), exact_dot(lift, spread))
-    uh, ul = split(padded(load_map, QB))
-    uu[0:QB, :] = uh
-    uu[QB:2 * QB, :] = ul
-
-    for copy in pair(out1, rim1, 0):
-        copy.wait_recv()
     put_table(list(rims(rim1)), 320)
-    for k in range(4):
-        gather_faces(k)
-    scale = STEP * jac_ref[...]
-    s1[...] = s1[...] + scale * change()
-
-    score = jnp.sum(column(odir_ref[...]) * s1[...], axis=0, keepdims=True)
-    opening = 0.2 * (jnp.maximum(score, 0.0) + jnp.log1p(jnp.exp(-jnp.abs(score))))
-    oh, ol = split(jnp.concatenate([opening[:, 128 * i:128 * i + 128] for i in range(16)], axis=0))
-    got = dot(jnp.concatenate([oh, ol], axis=0), elem_hot[...])
-    val[0:16, :] = got[0:16] + got[16:32]
-    sixteen = (iota((16, 128), 0) + 16).astype(F32)
-
-    def open_body(t, carry):
-        for r in range(4):
-            mine = sixteen == elem_row[1, pl.ds(4 * t + r, 1), :]
-            open_out[t, r:r + 1, :] = jnp.sum(
-                jnp.where(mine, val[0:16, lanes(4 * t + r)], 0.0), axis=0, keepdims=True)
-        return carry
-
-    lax.fori_loop(0, TILES, open_body, 0, unroll=2)
-    start_all(open_out, open_in, open_send, open_recv)
-
-    put_state(s1[...])
-    tr = traces()
-    put_table([tr], 0)
-    fill_outgoing(out2)
-    for copy in pair(out2, rim2, 2):
-        copy.start()
-
-    arrive_all(cells_out, cells_in, cell_send, cell_recv)
-
-    def cell_body(t, carry):
-        for r in range(4):
-            c = 4 * t + r
-            at = cells_in[t, r:r + 1, :].astype(I32)
-            cell_hi[:, lanes(c)] = ones_where(iota((128, 128), 0) == (at >> 7)).astype(BF16)
-            cell_lo[:, lanes(c)] = ones_where(iota((128, 128), 0) == (at & 127)).astype(BF16)
-        return carry
-
-    lax.fori_loop(0, TILES, cell_body, 0)
+    gather_faces(0)
+    gather_faces(1)
+
     arrive_all(open_out, open_in, open_send, open_recv)
 
-    def amount_body(t, carry):
-        for r in range(4):
-            c = 4 * t + r
-            high, rest = split(jnp.broadcast_to(open_in[t, r:r + 1, :], (128, 128)))
-            unit = cell_lo[:, lanes(c)]
-            vb[0:128, lanes(c)] = unit * high
-            vb[128:256, lanes(c)] = unit * rest
-        return carry
-
-    lax.fori_loop(0, TILES, amount_body, 0)
-    field = dot_nt(cell_hi[...], vb[...])
-    aper = base_ref[...] + (field[:, 0:128] + field[:, 128:256])
+    amounts = []
+    for t in range(TILES):
+        high = open_in[t].astype(BF16).astype(F32)
+        unit = cell_unit[:, 512 * t:512 * t + 512]
+        amounts.append(jnp.concatenate(
+            [unit * jnp.concatenate([jnp.broadcast_to(part, (16, 512)).astype(BF16)] * 4, axis=0)
+             for part in (high, open_in[t] - high)], axis=0))
+    field = dot_nt(jnp.concatenate(amounts, axis=1), cell_hot[...])
+    field = field[0:64] + field[64:128]
+    aper = base_ref[...] + jnp.concatenate([field[:, 0:128], field[:, 128:256]], axis=0)
     aper_ref[...] = aper
     c = aper * aper * aper / 12.0
     cond[...] = c
@@ -364,11 +395,15 @@
     for copy in edges(1):
         copy.start()
 
+    gather_faces(2)
+    gather_faces(3)
+    s1[...] = s1[...] + scale * change()
+
+    put_state(s1[...])
+    put_table([traces()], 0)
+    fill_outgoing(out2)
     for copy in pair(out2, rim2, 2):
-        copy.wait_recv()
-    put_table(list(rims(rim2)), 320)
-    gather_faces(0)
-
+        copy.start()
     p = press_ref[...]
     odd = (iota((128, 128), 0) & 1) == 1
     lane = iota((128, 128), 1)
@@ -400,34 +435,36 @@
     new_p = p + RATE * (inflow + inj_ref[...])
     new_press_ref[...] = new_p
 
-    ph, prest = split(new_p)
-    units = cell_lo[...]
-    val[...] = dot(jnp.concatenate([ph, prest], axis=1), jnp.concatenate([units, units], axis=0))
-
-    def press_body(t, carry):
-        for r in range(4):
-            mine = iota((128, 128), 0) == (cells_in[t, r:r + 1, :].astype(I32) >> 7)
-            press_out[t, r:r + 1, :] = jnp.sum(
-                jnp.where(mine, val[:, lanes(4 * t + r)], 0.0), axis=0, keepdims=True)
-        return carry
-
-    lax.fori_loop(0, TILES, press_body, 0)
+    ph, prest = split(jnp.concatenate([new_p[0:64], new_p[64:128]], axis=1))
+    pressures = jnp.concatenate([ph, prest], axis=0)
+    for b in range(4):
+        at = slice(2048 * b, 2048 * b + 2048)
+        got = dot(pressures, cell_hot[:, at])
+        mine = iota((64, 2048), 0) == cell_row[:, at]
+        picked = jnp.sum(jnp.where(mine, got[0:64] + got[64:128], 0.0), axis=0, keepdims=True)
+        for t in range(4):
+            press_out[4 * b + t] = picked[:, 512 * t:512 * t + 512]
     start_all(press_out, press_in, pr_send, pr_recv)
-    gather_faces(1)
-    gather_faces(2)
+
+    for k in range(4):
+        gather_own(k)
+
+    push = column(tdir_ref[...])
+    tau = exact_dot(tmap, push[0:Q])
+    of_facet = jnp.where(lax.div(iota((Q, 128), 0), 9) == lax.rem(iota((Q, 128), 1), 4), tau, 0.0)
+    spread = jnp.where(
+        lax.div(iota((Q, 128), 0), 9) == lax.div(iota((Q, 128), 1), 4), exact_dot(same, of_facet), 0.0)
+    load_map = jnp.where(
+        iota((Q, 128), 1) == 16, exact_dot(volume, push[0:Q]), exact_dot(lift, spread))
+    uh, ul = split(padded(load_map, QB))
+    uu[0:QB, :] = uh
+    uu[QB:2 * QB, :] = ul
     arrive_all(press_out, press_in, pr_send, pr_recv)
 
-    def load_body(t, carry):
-        for r in range(4):
-            c = 4 * t + r
-            mine = sixteen == elem_row[1, pl.ds(c, 1), :]
-            high, rest = split(jnp.where(mine, press_in[t, r:r + 1, :], 0.0))
-            va[0:16, lanes(c)] = high
-            va[16:32, lanes(c)] = rest
-        return carry
-
-    lax.fori_loop(0, TILES, load_body, 0, unroll=2)
-    load = dot_nt(va[0:32, :], elem_hot[...])
+    for t in range(TILES):
+        slot_row[:, 512 * t:512 * t + 512] = press_in[t]
+    high, rest = split(jnp.where(sixteen == elem_hi[...], slot_row[...], 0.0))
+    load = dot_nt(jnp.concatenate([high, rest], axis=0), elem_hot[...])
     load = load[0:16] + load[16:32]
     for i in range(16):
         lane_row[:, 128 * i:128 * i + 128] = load[i:i + 1]
@@ -442,8 +479,12 @@
             jnp.where(mine, got[:, HALO * side:HALO * side + HALO], 0.0), axis=0, keepdims=True)
     for copy in pair(wout, wrim, 4):
         copy.start()
-    gather_faces(3)
-    change1[...] = change()
+    for copy in pair(out2, rim2, 2):
+        copy.wait_recv()
+    put_table(list(rims(rim2)), 320)
+    for k in range(4):
+        gather_rims(k)
+    change2 = change()
     for copy in pair(wout, wrim, 4):
         copy.wait_recv()
     low, high_rim = rims(wrim)
@@ -461,7 +502,7 @@
     nh, nl = split(jnp.concatenate(near, axis=0))
     first = dot(uu[...], nh)
     extra = first[0:QP] + first[QB:QB + QP] + dot(uu[0:QB, :], nl)[0:QP]
-    result = s1[...] + push * w + scale * (change1[...] + extra)
+    result = s1[...] + push * w + scale * (change2 + extra)
     new_state_ref[...] = result[0:Q]
 
     for index, (outs, ins) in enumerate(((out1, rim1), (out2, rim2), (wout, wrim))):
@@ -487,6 +528,7 @@
     opening_dir, traction_dir, face_elem, face_tile, face_cell, face_count, pressure, base_aperture, injection,
 ):
     vmem = pl.BlockSpec(memory_space=pltpu.VMEM)
+    hbm = pl.BlockSpec(memory_space=pltpu.HBM)
     smem = pl.BlockSpec(memory_space=pltpu.SMEM)
     scratch = [
         pltpu.VMEM((QP, ELEMS), F32),
@@ -498,33 +540,51 @@
         pltpu.VMEM((2 * QB, 256), BF16),
         pltpu.VMEM((2 * QB, QB), BF16),
         pltpu.VMEM((2 * QB, 128), BF16),
+        pltpu.VMEM((32, QB), BF16),
+        pltpu.VMEM((2, 256, 128), F32),
         pltpu.VMEM((2, QP, HALO), F32),
         pltpu.VMEM((2, QP, HALO), F32),
         pltpu.VMEM((2, QP, HALO), F32),
         pltpu.VMEM((2, QP, HALO), F32),
         pltpu.VMEM((2, 1, HALO), F32),
         pltpu.VMEM((2, 1, HALO), F32),
+        pltpu.VMEM((128, SLOTS), BF16),
+        pltpu.VMEM((1, SLOTS), F32),
+        pltpu.VMEM((1, SLOTS), F32),
+        pltpu.VMEM((TILES, 1, 512), F32),
+        pltpu.VMEM((TILES, 1, 512), F32),
+        pltpu.VMEM((TILES, 1, 512), F32),
+        pltpu.VMEM((TILES, 1, 512), F32),
+        pltpu.VMEM((TILES, 1, 512), F32),
+        pltpu.VMEM((TILES, 1, 512), F32),
+        pltpu.VMEM((5, 64, 128), F32),
         pltpu.VMEM((256, SLOTS), BF16),
-        pltpu.VMEM((256, SLOTS), BF16),
-        pltpu.VMEM((128, SLOTS), BF16),
-        pltpu.VMEM((2, 64, 128), F32),
-        pltpu.VMEM((TILES, 4, 128), F32),
-        pltpu.VMEM((TILES, 4, 128), F32),
-        pltpu.VMEM((TILES, 4, 128), F32),
-        pltpu.VMEM((TILES, 4, 128), F32),
-        pltpu.VMEM((TILES, 4, 128), F32),
-        pltpu.VMEM((TILES, 4, 128), F32),
-        pltpu.VMEM((6, 64, 128), I32),
-        pltpu.VMEM((128, SLOTS), BF16),
-        pltpu.VMEM((128, SLOTS), BF16),
-        pltpu.VMEM((128, SLOTS), F32),
+        pltpu.VMEM((64, SLOTS), BF16),
+        pltpu.VMEM((1, SLOTS), I32),
         pltpu.VMEM((128, 128), F32),
         pltpu.VMEM((4, 64, 128), F32),
         pltpu.VMEM((4, 64, 128), F32),
         pltpu.VMEM((2, 128, 128), F32),
-        pltpu.VMEM((QP, ELEMS), F32),
+        pltpu.VMEM((4, QP, ELEMS), F32),
         pltpu.VMEM((1, ELEMS), F32),
-    ] + [pltpu.SemaphoreType.DMA((n,)) for n in (6, 6, 15, 15, 15, 15, 15, 15, 4, 4)]
+        pltpu.VMEM((1, SLOTS), F32),
+        pltpu.VMEM((Q, ELEMS), F32),
+        pltpu.VMEM((1, ELEMS), F32),
+        pltpu.VMEM((Q, Q), F32),
+        pltpu.VMEM((Q, Q), F32),
+        pltpu.VMEM((Q, Q), F32),
+        pltpu.VMEM((4, ELEMS), I32),
+        pltpu.VMEM((4, ELEMS), I32),
+        pltpu.VMEM((2, HALO), I32),
+        pltpu.VMEM((1, Q), F32),
+        pltpu.VMEM((1, Q), F32),
+        pltpu.VMEM((64, 128), I32),
+        pltpu.VMEM((64, 128), I32),
+        pltpu.VMEM((64, 128), I32),
+        pltpu.VMEM((128, 128), F32),
+        pltpu.VMEM((128, 128), F32),
+        pltpu.VMEM((128, 128), F32),
+    ] + [pltpu.SemaphoreType.DMA((n,)) for n in (16, 6, 6, 15, 15, 15, 15, 15, 15, 4, 4)]
     new_state, new_pressure, aperture = pl.pallas_call(
         kernel,
         out_shape=(
@@ -532,7 +592,7 @@
             jax.ShapeDtypeStruct((128, 128), F32),
             jax.ShapeDtypeStruct((128, 128), F32),
         ),
-        in_specs=[vmem] * 13 + [smem] + [vmem] * 3,
+        in_specs=[hbm] * 13 + [smem] + [hbm] * 3,
         out_specs=(vmem,) * 3,
         scratch_shapes=scratch,
         compiler_params=pltpu.CompilerParams(

time: 58.7 us -> 51.6 us (0.88)
  Pallas kernels: 54 us -> 46.8 us
    pallas_call x1, Pallas kernels: 54 us -> 46.8 us  [shards(): pl.pallas_call(kernel, out_shape=(jax.ShapeDtypeStruct((Q, ELEMS), F32),...]
where the time goes in v2:
time: 51.6 us; the launch traced here: 51.4 us
  Pallas kernels  46.8 us (91%)
  local copies, waits for them, and re-layouts  3.25 us (6%)
  between operations  1.3 us (3%)
    pallas_call x1, Pallas kernels, shards(): pl.pallas_call(kernel, out_shape=(jax.ShapeDtypeStruct((Q, ELEMS), F32),...  46.8 us
    unnamed x7, local copies, waits for them, and re-layouts  3.25 us

profile of v2, /device:TPU:1, one launch (start us, length us, event | category | flops | bytes accessed | tf_op | source)
XLA Modules:
  0.0 51.4 jit_solution(18068257484199084204)
XLA Ops:
  1.3 46.8 %shard_map.184 = (f32[36,2048]{1,0:T(8,128)}, f32[128,128]{1,0:T(8,128)}, f32[128,128]{1,0:T(8,128)}) custom-call(f32[36,2048]{1,0:T(8,128)} %state_hbm.1, f32[1,2048]{1,0:T(1,128)} %bitcast.39, f32[36,36]{1,0:T(8,128)} %stiff_hbm.1, f32[36,36]{1,0:T(8,128)} %tmap_hbm.1, f32[36,36]{1,0:T(8,128)} %lift_hbm.1, s32[4,2048]{1,0:T(4,128)} %nel_hbm.1, ...), custom_call_target="tpu_custom_call" | custom-call | tf_op jit(solution)/shard_map/pallas_call | solution.py:588
  48.1 0.0 copy-start.1
  48.1 1.8 %copy.29 = f32[36,2048]{1,0:T(8,128)} copy(f32[36,2048]{1,0:T(8,128)} %get-tuple-element.12) | data formatting | bytes 589824
  49.9 0.0 copy-done.1
  49.9 0.0 copy-start
  49.9 0.6 %copy.30 = f32[1,2,8192]{2,1,0:T(2,128)} copy(f32[1,2,8192]{2,1,0:T(2,128)S(1)} %bitcast.32) | data formatting | bytes 131072
  50.5 0.2 copy-done
  50.8 0.6 %copy.31 = f32[1,2,8192]{2,1,0:T(2,128)} copy(f32[1,2,8192]{2,1,0:T(2,128)S(1)} %bitcast.31) | data formatting | bytes 131072
Async XLA Ops:
  48.1 1.8 %copy-start.1 = (f32[128,128]{1,0:T(8,128)S(1)}, f32[128,128]{1,0:T(8,128)}, u32[]{:S(2)}) copy-start(f32[128,128]{1,0:T(8,128)} %get-tuple-element.7) | copy-start | bytes 196612
  49.9 0.9 %copy-start = (f32[128,128]{1,0:T(8,128)S(1)}, f32[128,128]{1,0:T(8,128)}, u32[]{:S(2)}) copy-start(f32[128,128]{1,0:T(8,128)} %get-tuple-element.8) | copy-start | bytes 196612

commit v3 on v2

--- a/solution.py
+++ b/solution.py
@@ -68,7 +68,7 @@
     state_hbm, jac_hbm, stiff_hbm, tmap_hbm, lift_hbm, nel_hbm, nfa_hbm, send_hbm, odir_hbm, tdir_hbm,
     fel_hbm, ftile_hbm, fcell_hbm, fcount_ref, press_hbm, base_hbm, inj_hbm,
     new_state_ref, new_press_ref, aper_ref,
-    s1, table, hot, send_hot, xh, xl, ww, tw, uu, gw, gtab, out1, out2, rim1, rim2, wout, wrim,
+    s1, table, hot, send_hot, xh, xl, ww, tw, uu, gw, gtab, out1, out2, rim1, rim2, wout, wrim, gout, grim,
     elem_hot, elem_hi, elem_lo, cells_out, cells_in, open_out, open_in, press_out, press_in,
     slot_tab, cell_hot, cell_unit, cell_row, cond, edge_out, edge_in, edge_wide, own2, lane_row, slot_row,
     state_ref, jac_ref, stiff_ref, tmap_ref, lift_ref, nel_ref, nfa_ref, send_ref, odir_ref, tdir_ref,
@@ -79,11 +79,11 @@
         pltpu.make_async_copy(source, target, in_sem.at[i])
         for i, (source, target) in enumerate((
             (state_hbm, state_ref), (tmap_hbm, tmap_ref), (send_hbm, send_ref), (lift_hbm, lift_ref),
-            (ftile_hbm, ftile_ref), (fcell_hbm, fcell_ref), (fel_hbm, fel_ref), (press_hbm, press_ref),
-            (nel_hbm, nel_ref), (nfa_hbm, nfa_ref), (stiff_hbm, stiff_ref), (odir_hbm, odir_ref),
+            (odir_hbm, odir_ref), (ftile_hbm, ftile_ref), (fcell_hbm, fcell_ref), (fel_hbm, fel_ref), (press_hbm, press_ref),
+            (nel_hbm, nel_ref), (nfa_hbm, nfa_ref), (stiff_hbm, stiff_ref),
             (jac_hbm, jac_ref), (tdir_hbm, tdir_ref), (base_hbm, base_ref), (inj_hbm, inj_ref)))
     ]
-    for load in loads[:4]:
+    for load in loads[:5]:
         load.start()
     rock = lax.axis_index("rock")
     plane = lax.axis_index("plane")
@@ -107,7 +107,7 @@
         return carry
 
     lax.fori_loop(1, TILES, greet, 0)
-    for load in loads[4:]:
+    for load in loads[5:]:
         load.start()
 
     def pair(outs, ins, index):
@@ -155,7 +155,7 @@
             return carry
         lax.fori_loop(1, TILES, one, 0)
 
-    for load in loads[:4]:
+    for load in loads[:5]:
         load.wait()
     tmap = tmap_ref[...]
     lift = lift_ref[...]
@@ -164,6 +164,25 @@
     tw[0:QB, :] = dot(th, widen).astype(BF16)
     tw[QB:2 * QB, :] = dot(tl, widen).astype(BF16)
 
+    same = ones_where(lax.rem(iota((Q, Q), 0), 9) == lax.rem(iota((Q, Q), 1), 9))
+    odir = odir_ref[...]
+    of_face = jnp.where(lax.div(iota((16, Q), 0), 4) == lax.div(iota((16, Q), 1), 9), exact_dot(odir, lift), 0.0)
+    of_face = exact_dot(of_face, same)
+    gh, gl = split(jnp.where(lax.rem(iota((16, Q), 0), 4) == lax.div(iota((16, Q), 1), 9), of_face, 0.0))
+    gw[0:16, :] = dot(gh, widen).astype(BF16)
+    gw[16:32, :] = dot(gl, widen).astype(BF16)
+
+    def scores_of(x):
+        high, rest = split(padded(x, QB))
+        got = dot(gw[...], high)
+        return got[0:16] + got[16:32] + dot(gw[0:16, :], rest)
+
+    def put_scores(got, start):
+        for l in range(got.shape[1] // 256):
+            for half in range(2):
+                at = 256 * l + 128 * half
+                gtab[half, pl.ds(start + l, 16, stride=16), :] = got[:, at:at + 128]
+
     def put_state(x):
         high, rest = split(padded(x, QB))
         xh[0:QB, :] = high
@@ -231,10 +250,12 @@
     for side in range(2):
         send_hot[:, HALO * side:HALO * side + HALO] = units(256, send_ref[side:side + 1, :] & 255)
     fill_outgoing(out1)
+    for side in range(2):
+        gout[side] = scores_of(out1[side])
     pl.semaphore_wait(barrier, TILES + 1)
-    for copy in pair(out1, rim1, 0):
+    for copy in pair(gout, grim, 6) + pair(out1, rim1, 0):
         copy.start()
-    for load in loads[4:]:
+    for load in loads[5:]:
         load.wait()
     edge_out[0] = press_ref[pl.ds(0, 64, stride=2), :]
     edge_out[1] = press_ref[pl.ds(1, 64, stride=2), :]
@@ -303,34 +324,16 @@
         elem_hot[:, at] = units(128, elem_lo[:, at].astype(I32))
 
     volume = stiff_ref[...] - exact_dot(lift, tmap)
-    same = ones_where(lax.rem(iota((Q, Q), 0), 9) == lax.rem(iota((Q, Q), 1), 9))
-    odir = odir_ref[...]
-    of_face = jnp.where(lax.div(iota((16, Q), 0), 4) == lax.div(iota((16, Q), 1), 9), exact_dot(odir, lift), 0.0)
-    of_face = exact_dot(of_face, same)
-    gh, gl = split(jnp.where(lax.rem(iota((16, Q), 0), 4) == lax.div(iota((16, Q), 1), 9), of_face, 0.0))
-    gw[0:16, :] = dot(gh, widen).astype(BF16)
-    gw[16:32, :] = dot(gl, widen).astype(BF16)
-
-    def put_scores(parts, start):
-        for x in parts:
-            high, rest = split(padded(x, QB))
-            got = dot(gw[...], high)
-            got = got[0:16] + got[16:32] + dot(gw[0:16, :], rest)
-            for l in range(x.shape[1] // 256):
-                for half in range(2):
-                    at = 256 * l + 128 * half
-                    gtab[half, pl.ds(start + l, 16, stride=16), :] = got[:, at:at + 128]
-            start += x.shape[1] // 256
-
-    put_scores([tr], 0)
+    put_scores(scores_of(tr), 0)
     scale = STEP * jac_ref[...]
     own_state = s1[...]
     direct = jnp.sum(column(odir) * own_state, axis=0, keepdims=True)
     within = jnp.sum(column(exact_dot(odir, volume)) * own_state, axis=0, keepdims=True)
 
-    for copy in pair(out1, rim1, 0):
+    for copy in pair(gout, grim, 6):
         copy.wait_recv()
-    put_scores(rims(rim1), 8)
+    for side, got in enumerate(rims(grim)):
+        put_scores(got, 8 + 4 * side)
     for k in range(4):
         at = slice(64 * k, 64 * k + 64)
         gh, gl = split(jnp.concatenate([gtab[0, at, :], gtab[1, at, :]], axis=1))
@@ -371,6 +374,8 @@
     ww[QB:2 * QB, :] = (dot(ml, own_block) + dot(ll, face_block)).astype(BF16)
     xh[5 * QB:256, :] = jnp.zeros((16, ELEMS), BF16)
     xl[5 * QB:256, :] = jnp.zeros((16, ELEMS), BF16)
+    for copy in pair(out1, rim1, 0):
+        copy.wait_recv()
     put_table(list(rims(rim1)), 320)
     gather_faces(0)
     gather_faces(1)
@@ -505,7 +510,7 @@
     result = s1[...] + push * w + scale * (change2 + extra)
     new_state_ref[...] = result[0:Q]
 
-    for index, (outs, ins) in enumerate(((out1, rim1), (out2, rim2), (wout, wrim))):
+    for index, (outs, ins) in enumerate(((out1, rim1), (out2, rim2), (wout, wrim), (gout, grim))):
         for copy in pair(outs, ins, 2 * index):
             copy.wait_send()
     for copy in edges(0) + edges(1):
@@ -513,6 +518,19 @@
     sent_all(cells_out, cells_in, cell_send, cell_recv)
     sent_all(open_out, open_in, open_send, open_recv)
     sent_all(press_out, press_in, pr_send, pr_recv)
+
+
+def hand_over(*refs):
+    sources, targets, held, sems = refs[0:3], refs[3:6], refs[6:9], refs[9]
+    arrive = [pltpu.make_async_copy(sources[i], held[i], sems.at[i]) for i in range(3)]
+    leave = [pltpu.make_async_copy(held[i], targets[i], sems.at[3 + i]) for i in range(3)]
+    for copy in arrive:
+        copy.start()
+    for first, then in zip(arrive, leave):
+        first.wait()
+        then.start()
+    for copy in leave:
+        copy.wait()
 
 
 def interleaved(x):
@@ -548,6 +566,8 @@
         pltpu.VMEM((2, QP, HALO), F32),
         pltpu.VMEM((2, 1, HALO), F32),
         pltpu.VMEM((2, 1, HALO), F32),
+        pltpu.VMEM((2, 16, HALO), F32),
+        pltpu.VMEM((2, 16, HALO), F32),
         pltpu.VMEM((128, SLOTS), BF16),
         pltpu.VMEM((1, SLOTS), F32),
         pltpu.VMEM((1, SLOTS), F32),
@@ -584,7 +604,7 @@
         pltpu.VMEM((128, 128), F32),
         pltpu.VMEM((128, 128), F32),
         pltpu.VMEM((128, 128), F32),
-    ] + [pltpu.SemaphoreType.DMA((n,)) for n in (16, 6, 6, 15, 15, 15, 15, 15, 15, 4, 4)]
+    ] + [pltpu.SemaphoreType.DMA((n,)) for n in (16, 8, 8, 15, 15, 15, 15, 15, 15, 4, 4)]
     new_state, new_pressure, aperture = pl.pallas_call(
         kernel,
         out_shape=(
@@ -603,6 +623,14 @@
         face_tile.reshape(64, 128), face_cell.reshape(64, 128), face_count, interleaved(pressure),
         interleaved(base_aperture), interleaved(injection),
     )
+    results = (new_state, new_pressure, aperture)
+    new_state, new_pressure, aperture = pl.pallas_call(
+        hand_over,
+        out_shape=tuple(jax.ShapeDtypeStruct(x.shape, F32) for x in results),
+        in_specs=[hbm] * 3,
+        out_specs=(hbm,) * 3,
+        scratch_shapes=[pltpu.VMEM(x.shape, F32) for x in results] + [pltpu.SemaphoreType.DMA((6,))],
+    )(*results)
     return new_state, straight(new_pressure), straight(aperture)
 
 

time: 51.6 us -> 49.9 us (0.967)
  local copies, waits for them, and re-layouts: 3.25 us -> 0 us
  Pallas kernels: 46.8 us -> 48.3 us
    unnamed x7 -> x0, local copies, waits for them, and re-layouts: 3.25 us -> none
    pallas_call x0 -> x1, Pallas kernels: none -> 1.78 us  [shards(): pl.pallas_call(hand_over, out_shape=tuple((jax.ShapeDtypeStruct(x.shape,...]
where the time goes in v3:
time: 49.9 us; the launch traced here: 49.7 us
  Pallas kernels  48.3 us (97%)
  between operations  1.47 us (3%)
    pallas_call x1, Pallas kernels, shards(): pl.pallas_call(kernel, out_shape=(jax.ShapeDtypeStruct((Q, ELEMS), F32),...  46.5 us
    pallas_call x1, Pallas kernels, shards(): pl.pallas_call(hand_over, out_shape=tuple((jax.ShapeDtypeStruct(x.shape,...  1.78 us

profile of v3, /device:TPU:1, one launch (start us, length us, event | category | flops | bytes accessed | tf_op | source)
XLA Modules:
  0.0 49.7 jit_solution(6592592516234739289)
XLA Ops:
  1.3 46.5 %shard_map.184 = (f32[36,2048]{1,0:T(8,128)}, f32[128,128]{1,0:T(8,128)}, f32[128,128]{1,0:T(8,128)}) custom-call(f32[36,2048]{1,0:T(8,128)} %state_hbm.1, f32[1,2048]{1,0:T(1,128)} %bitcast.37, f32[36,36]{1,0:T(8,128)} %stiff_hbm.1, f32[36,36]{1,0:T(8,128)} %tmap_hbm.1, f32[36,36]{1,0:T(8,128)} %lift_hbm.1, s32[4,2048]{1,0:T(4,128)} %nel_hbm.1, ...), custom_call_target="tpu_custom_call" | custom-call | tf_op jit(solution)/shard_map/pallas_call | solution.py:608
  47.8 1.8 %shard_map.185 = (f32[36,2048]{1,0:T(8,128)}, f32[128,128]{1,0:T(8,128)}, f32[128,128]{1,0:T(8,128)}) custom-call(f32[36,2048]{1,0:T(8,128)} %get-tuple-element.9.refs_0_, f32[128,128]{1,0:T(8,128)} %get-tuple-element.10.refs_1_, f32[128,128]{1,0:T(8,128)} %get-tuple-element.11.refs_2_), custom_call_target="tpu_custom_call" | custom-call | tf_op jit(solution)/shard_map/pallas_call | solution.py:627

commit v4 on v3

--- a/solution.py
+++ b/solution.py
@@ -19,6 +19,9 @@
 SLOTS = 8192
 TILES = 16
 PARTS = 128
+FAR = [(a, b) for a in (1, 2, 3) for b in (1, 2, 3)]
+NEAR = [(0, 1), (0, 2), (0, 3), (1, 0), (2, 0), (3, 0)]
+STEPS = FAR + NEAR
 
 
 def dot(a, b):
@@ -70,7 +73,7 @@
     new_state_ref, new_press_ref, aper_ref,
     s1, table, hot, send_hot, xh, xl, ww, tw, uu, gw, gtab, out1, out2, rim1, rim2, wout, wrim, gout, grim,
     elem_hot, elem_hi, elem_lo, cells_out, cells_in, open_out, open_in, press_out, press_in,
-    slot_tab, cell_hot, cell_unit, cell_row, cond, edge_out, edge_in, edge_wide, own2, lane_row, slot_row,
+    slot_tab, cell_hot, cell_unit, cell_row, cond, edge_out, edge_in, edge_wide, own2, lane_row,
     state_ref, jac_ref, stiff_ref, tmap_ref, lift_ref, nel_ref, nfa_ref, send_ref, odir_ref, tdir_ref,
     fel_ref, ftile_ref, fcell_ref, press_ref, base_ref, inj_ref, in_sem,
     halo_send, halo_recv, cell_send, cell_recv, open_send, open_recv, pr_send, pr_recv, edge_send, edge_recv,
@@ -83,8 +86,7 @@
             (nel_hbm, nel_ref), (nfa_hbm, nfa_ref), (stiff_hbm, stiff_ref),
             (jac_hbm, jac_ref), (tdir_hbm, tdir_ref), (base_hbm, base_ref), (inj_hbm, inj_ref)))
     ]
-    for load in loads[:5]:
-        load.start()
+    loads[0].start()
     rock = lax.axis_index("rock")
     plane = lax.axis_index("plane")
     here = rock * TILES + plane
@@ -95,19 +97,21 @@
     next_tile = (rock, lax.rem(plane + 1, TILES))
     prev_tile = (rock, lax.rem(plane + TILES - 1, TILES))
 
-    def peer(o):
-        return lax.rem(plane + o, TILES)
+    def tile_at(a, b):
+        return lax.rem(lax.div(plane, 4) + a, 4) * 4 + lax.rem(lax.rem(plane, 4) + b, 4)
+
+    targets = [tile_at(a, b) for a, b in STEPS]
+    sources = [tile_at(4 - a, 4 - b) for a, b in STEPS]
+    far_tiles = sources[:len(FAR)]
+    near_tiles = [plane] + sources[len(FAR):]
 
     barrier = pltpu.get_barrier_semaphore()
     for target in (next_part, prev_part):
         pl.semaphore_signal(barrier, inc=1, device_id=target, device_id_type=MESH)
 
-    def greet(o, carry):
-        pl.semaphore_signal(barrier, inc=1, device_id=(rock, peer(o)), device_id_type=MESH)
-        return carry
-
-    lax.fori_loop(1, TILES, greet, 0)
-    for load in loads[5:]:
+    for target in targets:
+        pl.semaphore_signal(barrier, inc=1, device_id=(rock, target), device_id_type=MESH)
+    for load in loads[1:]:
         load.start()
 
     def pair(outs, ins, index):
@@ -132,28 +136,26 @@
 
     def swap(outs, ins, sends, recvs, o):
         return pltpu.make_async_remote_copy(
-            outs.at[peer(o)], ins.at[plane], sends.at[o - 1], recvs.at[o - 1],
-            device_id=(rock, peer(o)), device_id_type=MESH)
+            outs.at[targets[o]], ins.at[plane], sends.at[o], recvs.at[o],
+            device_id=(rock, targets[o]), device_id_type=MESH)
 
     def start_all(*what):
-        def one(o, carry):
+        for o in range(len(STEPS)):
             swap(*what, o).start()
-            return carry
-        lax.fori_loop(1, TILES, one, 0)
         outs, ins = what[:2]
         ins[plane] = outs[plane]
 
-    def arrive_all(*what):
-        def one(o, carry):
+    def arrive_far(*what):
+        for o in range(len(FAR)):
             swap(*what, o).wait_recv()
-            return carry
-        lax.fori_loop(1, TILES, one, 0)
+
+    def arrive_near(*what):
+        for o in range(len(FAR), len(STEPS)):
+            swap(*what, o).wait_recv()
 
     def sent_all(*what):
-        def one(o, carry):
+        for o in range(len(STEPS)):
             swap(*what, o).wait_send()
-            return carry
-        lax.fori_loop(1, TILES, one, 0)
 
     for load in loads[:5]:
         load.wait()
@@ -194,29 +196,33 @@
 
     def put_table(parts, start):
         rows = jnp.concatenate(
-            [x[:, 256 * l:256 * l + 256] for x in parts for l in range(x.shape[1] // 256)], axis=0)
+            [x[0:Q, 256 * l:256 * l + 256] for x in parts for l in range(x.shape[1] // 256)], axis=0)
         high, rest = split(rows)
         table[start:start + rows.shape[0], 0:256] = high
         table[start:start + rows.shape[0], 256:512] = rest
 
     def pick(got, rows, which, first, count):
-        for l in range(count):
-            part = rows[QP * l:QP * l + QP]
-            got = part if got is None else jnp.where(which == first + l, part, got)
+        for l in range(count // 2):
+            part = rows[2 * Q * l:2 * Q * l + 2 * Q]
+            got = part if got is None else jnp.where((which >> 1) == first // 2 + l, part, got)
         return got
+
+    def one_of(got, which):
+        return jnp.where((which & 1) == 1, got[Q:2 * Q], got[0:Q])
 
     def fill_outgoing(out):
         for side in range(2):
             a = send_hot[:, HALO * side:HALO * side + HALO]
-            rows = dot(table[0:320, :], jnp.concatenate([a, a], axis=0))
-            out[side] = pick(None, rows, send_ref[side:side + 1, :] >> 8, 0, 8)
+            which = send_ref[side:side + 1, :] >> 8
+            rows = dot(table[0:8 * Q, :], jnp.concatenate([a, a], axis=0))
+            out[side] = padded(one_of(pick(None, rows, which, 0, 8), which), QP)
 
     def rims(rim):
         lower = jnp.where(here > 0, rim[0], 0.0)
         upper = jnp.where(here < PARTS - 1, rim[1], 0.0)
         return lower, upper
 
-    face_of_row = lax.div(iota((QP, 1), 0), 9)
+    face_of_row = lax.div(iota((Q, 1), 0), 9)
 
     def columns(k, rows):
         a = hot[:, ELEMS * k:ELEMS * k + ELEMS]
@@ -229,13 +235,15 @@
         xl[QB * (k + 1):QB * (k + 2), :] = rest
 
     def gather_faces(k):
-        put_faces(k, pick(None, columns(k, table[...]), nel_ref[k:k + 1, :] >> 8, 0, 16))
+        which = nel_ref[k:k + 1, :] >> 8
+        put_faces(k, one_of(pick(None, columns(k, table[...]), which, 0, 16), which))
 
     def gather_own(k):
-        own2[k] = pick(None, columns(k, table[0:320, :]), nel_ref[k:k + 1, :] >> 8, 0, 8)
+        own2[k] = pick(None, columns(k, table[0:8 * Q, :]), nel_ref[k:k + 1, :] >> 8, 0, 8)
 
     def gather_rims(k):
-        put_faces(k, pick(own2[k], columns(k, table[320:640, :]), nel_ref[k:k + 1, :] >> 8, 8, 8))
+        which = nel_ref[k:k + 1, :] >> 8
+        put_faces(k, one_of(pick(own2[k], columns(k, table[8 * Q:, :]), which, 8, 8), which))
 
     def change():
         first = dot(ww[...], xh[...])
@@ -352,7 +360,8 @@
         open_out[t] = picked[:, 512 * t:512 * t + 512]
     start_all(open_out, open_in, open_send, open_recv)
 
-    arrive_all(cells_out, cells_in, cell_send, cell_recv)
+    arrive_near(cells_out, cells_in, cell_send, cell_recv)
+    arrive_far(cells_out, cells_in, cell_send, cell_recv)
 
     for t in range(TILES):
         at = slice(512 * t, 512 * t + 512)
@@ -376,20 +385,26 @@
     xl[5 * QB:256, :] = jnp.zeros((16, ELEMS), BF16)
     for copy in pair(out1, rim1, 0):
         copy.wait_recv()
-    put_table(list(rims(rim1)), 320)
+    put_table(list(rims(rim1)), 8 * Q)
     gather_faces(0)
-    gather_faces(1)
-
-    arrive_all(open_out, open_in, open_send, open_recv)
-
-    amounts = []
-    for t in range(TILES):
-        high = open_in[t].astype(BF16).astype(F32)
-        unit = cell_unit[:, 512 * t:512 * t + 512]
-        amounts.append(jnp.concatenate(
-            [unit * jnp.concatenate([jnp.broadcast_to(part, (16, 512)).astype(BF16)] * 4, axis=0)
-             for part in (high, open_in[t] - high)], axis=0))
-    field = dot_nt(jnp.concatenate(amounts, axis=1), cell_hot[...])
+
+    def field_of(tiles):
+        amounts = []
+        for t in tiles:
+            got = open_in[t]
+            high = got.astype(BF16).astype(F32)
+            unit = cell_unit[:, lanes(t, 512)]
+            amounts.append(jnp.concatenate(
+                [unit * jnp.concatenate([jnp.broadcast_to(part, (16, 512)).astype(BF16)] * 4, axis=0)
+                 for part in (high, got - high)], axis=0))
+        return dot_nt(
+            jnp.concatenate(amounts, axis=1),
+            jnp.concatenate([cell_hot[:, lanes(t, 512)] for t in tiles], axis=1))
+
+    arrive_near(open_out, open_in, open_send, open_recv)
+    field = field_of(near_tiles)
+    arrive_far(open_out, open_in, open_send, open_recv)
+    field = field + field_of(far_tiles)
     field = field[0:64] + field[64:128]
     aper = base_ref[...] + jnp.concatenate([field[:, 0:128], field[:, 128:256]], axis=0)
     aper_ref[...] = aper
@@ -400,15 +415,10 @@
     for copy in edges(1):
         copy.start()
 
-    gather_faces(2)
-    gather_faces(3)
+    for k in range(1, 4):
+        gather_faces(k)
     s1[...] = s1[...] + scale * change()
 
-    put_state(s1[...])
-    put_table([traces()], 0)
-    fill_outgoing(out2)
-    for copy in pair(out2, rim2, 2):
-        copy.start()
     p = press_ref[...]
     odd = (iota((128, 128), 0) & 1) == 1
     lane = iota((128, 128), 1)
@@ -451,6 +461,11 @@
             press_out[4 * b + t] = picked[:, 512 * t:512 * t + 512]
     start_all(press_out, press_in, pr_send, pr_recv)
 
+    put_state(s1[...])
+    put_table([traces()], 0)
+    fill_outgoing(out2)
+    for copy in pair(out2, rim2, 2):
+        copy.start()
     for k in range(4):
         gather_own(k)
 
@@ -464,12 +479,18 @@
     uh, ul = split(padded(load_map, QB))
     uu[0:QB, :] = uh
     uu[QB:2 * QB, :] = ul
-    arrive_all(press_out, press_in, pr_send, pr_recv)
-
-    for t in range(TILES):
-        slot_row[:, 512 * t:512 * t + 512] = press_in[t]
-    high, rest = split(jnp.where(sixteen == elem_hi[...], slot_row[...], 0.0))
-    load = dot_nt(jnp.concatenate([high, rest], axis=0), elem_hot[...])
+
+    def load_of(tiles):
+        high, rest = split(jnp.concatenate(
+            [jnp.where(sixteen == elem_hi[:, lanes(t, 512)], press_in[t], 0.0) for t in tiles], axis=1))
+        return dot_nt(
+            jnp.concatenate([high, rest], axis=0),
+            jnp.concatenate([elem_hot[:, lanes(t, 512)] for t in tiles], axis=1))
+
+    arrive_near(press_out, press_in, pr_send, pr_recv)
+    load = load_of(near_tiles)
+    arrive_far(press_out, press_in, pr_send, pr_recv)
+    load = load + load_of(far_tiles)
     load = load[0:16] + load[16:32]
     for i in range(16):
         lane_row[:, 128 * i:128 * i + 128] = load[i:i + 1]
@@ -486,7 +507,7 @@
         copy.start()
     for copy in pair(out2, rim2, 2):
         copy.wait_recv()
-    put_table(list(rims(rim2)), 320)
+    put_table(list(rims(rim2)), 8 * Q)
     for k in range(4):
         gather_rims(k)
     change2 = change()
@@ -521,15 +542,10 @@
 
 
 def hand_over(*refs):
-    sources, targets, held, sems = refs[0:3], refs[3:6], refs[6:9], refs[9]
-    arrive = [pltpu.make_async_copy(sources[i], held[i], sems.at[i]) for i in range(3)]
-    leave = [pltpu.make_async_copy(held[i], targets[i], sems.at[3 + i]) for i in range(3)]
-    for copy in arrive:
+    copies = [pltpu.make_async_copy(refs[i], refs[3 + i], refs[6].at[i]) for i in range(3)]
+    for copy in copies:
         copy.start()
-    for first, then in zip(arrive, leave):
-        first.wait()
-        then.start()
-    for copy in leave:
+    for copy in copies:
         copy.wait()
 
 
@@ -550,7 +566,7 @@
     smem = pl.BlockSpec(memory_space=pltpu.SMEM)
     scratch = [
         pltpu.VMEM((QP, ELEMS), F32),
-        pltpu.VMEM((640, 512), BF16),
+        pltpu.VMEM((16 * Q, 512), BF16),
         pltpu.VMEM((256, SLOTS), BF16),
         pltpu.VMEM((256, 2 * HALO), BF16),
         pltpu.VMEM((256, ELEMS), BF16),
@@ -585,9 +601,8 @@
         pltpu.VMEM((4, 64, 128), F32),
         pltpu.VMEM((4, 64, 128), F32),
         pltpu.VMEM((2, 128, 128), F32),
-        pltpu.VMEM((4, QP, ELEMS), F32),
+        pltpu.VMEM((4, 2 * Q, ELEMS), F32),
         pltpu.VMEM((1, ELEMS), F32),
-        pltpu.VMEM((1, SLOTS), F32),
         pltpu.VMEM((Q, ELEMS), F32),
         pltpu.VMEM((1, ELEMS), F32),
         pltpu.VMEM((Q, Q), F32),
@@ -608,9 +623,9 @@
     new_state, new_pressure, aperture = pl.pallas_call(
         kernel,
         out_shape=(
-            jax.ShapeDtypeStruct((Q, ELEMS), F32),
-            jax.ShapeDtypeStruct((128, 128), F32),
-            jax.ShapeDtypeStruct((128, 128), F32),
+            pltpu.VMEM((Q, ELEMS), F32),
+            pltpu.VMEM((128, 128), F32),
+            pltpu.VMEM((128, 128), F32),
         ),
         in_specs=[hbm] * 13 + [smem] + [hbm] * 3,
         out_specs=(vmem,) * 3,
@@ -627,9 +642,10 @@
     new_state, new_pressure, aperture = pl.pallas_call(
         hand_over,
         out_shape=tuple(jax.ShapeDtypeStruct(x.shape, F32) for x in results),
-        in_specs=[hbm] * 3,
+        in_specs=[vmem] * 3,
         out_specs=(hbm,) * 3,
-        scratch_shapes=[pltpu.VMEM(x.shape, F32) for x in results] + [pltpu.SemaphoreType.DMA((6,))],
+        scratch_shapes=[pltpu.SemaphoreType.DMA((3,))],
+        compiler_params=pltpu.CompilerParams(vmem_limit_bytes=2**20),
     )(*results)
     return new_state, straight(new_pressure), straight(aperture)
 

time: 49.9 us -> 46.4 us (0.930)
  Pallas kernels: 48.3 us -> 44.4 us
    pallas_call x1, Pallas kernels: 46.5 us -> 43.6 us  [shards(): pl.pallas_call(kernel, out_shape=(pltpu.VMEM((Q, ELEMS), F32), pltpu.VMEM...]
    pallas_call x1, Pallas kernels: 1.78 us -> 0.79 us  [shards(): pl.pallas_call(hand_over, out_shape=tuple((jax.ShapeDtypeStruct(x.shape,...]
where the time goes in v4:
time: 46.4 us; the launch traced here: 45.9 us
  Pallas kernels  44.4 us (96%)
  between operations  1.47 us (3%)
    pallas_call x1, Pallas kernels, shards(): pl.pallas_call(kernel, out_shape=(pltpu.VMEM((Q, ELEMS), F32), pltpu.VMEM...  43.6 us

profile of v4, /device:TPU:1, one launch (start us, length us, event | category | flops | bytes accessed | tf_op | source)
XLA Modules:
  0.0 45.9 jit_solution(8057019232555461687)
XLA Ops:
  1.3 43.6 %shard_map.184 = (f32[36,2048]{1,0:T(8,128)S(1)}, f32[128,128]{1,0:T(8,128)S(1)}, f32[128,128]{1,0:T(8,128)S(1)}) custom-call(f32[36,2048]{1,0:T(8,128)} %state_hbm.1, f32[1,2048]{1,0:T(1,128)} %bitcast.37, f32[36,36]{1,0:T(8,128)} %stiff_hbm.1, f32[36,36]{1,0:T(8,128)} %tmap_hbm.1, f32[36,36]{1,0:T(8,128)} %lift_hbm.1, s32[4,2048]{1,0:T(4,128)} %nel_hbm.1, ...), custom_call_target="tpu_custom_call" | custom-call | tf_op jit(solution)/shard_map/pallas_call | solution.py:623
  44.9 0.8 %shard_map.185 = (f32[36,2048]{1,0:T(8,128)}, f32[128,128]{1,0:T(8,128)}, f32[128,128]{1,0:T(8,128)}) custom-call(f32[36,2048]{1,0:T(8,128)S(1)} %get-tuple-element.9.refs_0_, f32[128,128]{1,0:T(8,128)S(1)} %get-tuple-element.10.refs_1_, f32[128,128]{1,0:T(8,128)S(1)} %get-tuple-element.11.refs_2_), custom_call_target="tpu_custom_call" | custom-call | tf_op jit(solution)/shard_map/pallas_call | solution.py:642

commit v5 on v4

--- a/solution.py
+++ b/solution.py
@@ -106,11 +106,15 @@
     near_tiles = [plane] + sources[len(FAR):]
 
     barrier = pltpu.get_barrier_semaphore()
-    for target in (next_part, prev_part):
+
+    def greet(target):
         pl.semaphore_signal(barrier, inc=1, device_id=target, device_id_type=MESH)
 
+    pl.when(here < PARTS - 1)(lambda: greet(next_part))
+    pl.when(here > 0)(lambda: greet(prev_part))
+
     for target in targets:
-        pl.semaphore_signal(barrier, inc=1, device_id=(rock, target), device_id_type=MESH)
+        greet((rock, target))
     for load in loads[1:]:
         load.start()
 
@@ -124,6 +128,31 @@
                 device_id=next_part, device_id_type=MESH),
         ]
 
+    def start_pair(*what):
+        down, up = pair(*what)
+        pl.when(here > 0)(down.start)
+        pl.when(here < PARTS - 1)(up.start)
+
+    def arrive_pair(*what):
+        down, up = pair(*what)
+        pl.when(here < PARTS - 1)(down.wait_recv)
+        pl.when(here > 0)(up.wait_recv)
+
+    def sent_pair(*what):
+        down, up = pair(*what)
+        pl.when(here > 0)(down.wait_send)
+        pl.when(here < PARTS - 1)(up.wait_send)
+
+    @pl.when(here == 0)
+    def _():
+        for rim in (grim, rim1, rim2, wrim):
+            rim[0] = jnp.zeros(rim.shape[1:], F32)
+
+    @pl.when(here == PARTS - 1)
+    def _():
+        for rim in (grim, rim1, rim2, wrim):
+            rim[1] = jnp.zeros(rim.shape[1:], F32)
+
     def edges(index):
         return [
             pltpu.make_async_remote_copy(
@@ -217,11 +246,6 @@
             rows = dot(table[0:8 * Q, :], jnp.concatenate([a, a], axis=0))
             out[side] = padded(one_of(pick(None, rows, which, 0, 8), which), QP)
 
-    def rims(rim):
-        lower = jnp.where(here > 0, rim[0], 0.0)
-        upper = jnp.where(here < PARTS - 1, rim[1], 0.0)
-        return lower, upper
-
     face_of_row = lax.div(iota((Q, 1), 0), 9)
 
     def columns(k, rows):
@@ -260,9 +284,10 @@
     fill_outgoing(out1)
     for side in range(2):
         gout[side] = scores_of(out1[side])
-    pl.semaphore_wait(barrier, TILES + 1)
-    for copy in pair(gout, grim, 6) + pair(out1, rim1, 0):
-        copy.start()
+    both = lax.div(here + PARTS - 2, PARTS - 1) + lax.div(2 * PARTS - 3 - here, PARTS - 1)
+    pl.semaphore_wait(barrier, TILES - 1 + both)
+    start_pair(gout, grim, 6)
+    start_pair(out1, rim1, 0)
     for load in loads[5:]:
         load.wait()
     edge_out[0] = press_ref[pl.ds(0, 64, stride=2), :]
@@ -338,10 +363,9 @@
     direct = jnp.sum(column(odir) * own_state, axis=0, keepdims=True)
     within = jnp.sum(column(exact_dot(odir, volume)) * own_state, axis=0, keepdims=True)
 
-    for copy in pair(gout, grim, 6):
-        copy.wait_recv()
-    for side, got in enumerate(rims(grim)):
-        put_scores(got, 8 + 4 * side)
+    arrive_pair(gout, grim, 6)
+    for side in range(2):
+        put_scores(grim[side], 8 + 4 * side)
     for k in range(4):
         at = slice(64 * k, 64 * k + 64)
         gh, gl = split(jnp.concatenate([gtab[0, at, :], gtab[1, at, :]], axis=1))
@@ -383,9 +407,8 @@
     ww[QB:2 * QB, :] = (dot(ml, own_block) + dot(ll, face_block)).astype(BF16)
     xh[5 * QB:256, :] = jnp.zeros((16, ELEMS), BF16)
     xl[5 * QB:256, :] = jnp.zeros((16, ELEMS), BF16)
-    for copy in pair(out1, rim1, 0):
-        copy.wait_recv()
-    put_table(list(rims(rim1)), 8 * Q)
+    arrive_pair(out1, rim1, 0)
+    put_table([rim1[0], rim1[1]], 8 * Q)
     gather_faces(0)
 
     def field_of(tiles):
@@ -464,21 +487,10 @@
     put_state(s1[...])
     put_table([traces()], 0)
     fill_outgoing(out2)
-    for copy in pair(out2, rim2, 2):
-        copy.start()
+    start_pair(out2, rim2, 2)
     for k in range(4):
         gather_own(k)
 
-    push = column(tdir_ref[...])
-    tau = exact_dot(tmap, push[0:Q])
-    of_facet = jnp.where(lax.div(iota((Q, 128), 0), 9) == lax.rem(iota((Q, 128), 1), 4), tau, 0.0)
-    spread = jnp.where(
-        lax.div(iota((Q, 128), 0), 9) == lax.div(iota((Q, 128), 1), 4), exact_dot(same, of_facet), 0.0)
-    load_map = jnp.where(
-        iota((Q, 128), 1) == 16, exact_dot(volume, push[0:Q]), exact_dot(lift, spread))
-    uh, ul = split(padded(load_map, QB))
-    uu[0:QB, :] = uh
-    uu[QB:2 * QB, :] = ul
 
     def load_of(tiles):
         high, rest = split(jnp.concatenate(
@@ -503,18 +515,24 @@
         mine = iota((8, HALO), 0) == (send_ref[side:side + 1, :] >> 8)
         wout[side] = jnp.sum(
             jnp.where(mine, got[:, HALO * side:HALO * side + HALO], 0.0), axis=0, keepdims=True)
-    for copy in pair(wout, wrim, 4):
-        copy.start()
-    for copy in pair(out2, rim2, 2):
-        copy.wait_recv()
-    put_table(list(rims(rim2)), 8 * Q)
+    start_pair(wout, wrim, 4)
+    push = column(tdir_ref[...])
+    tau = exact_dot(tmap, push[0:Q])
+    of_facet = jnp.where(lax.div(iota((Q, 128), 0), 9) == lax.rem(iota((Q, 128), 1), 4), tau, 0.0)
+    spread = jnp.where(
+        lax.div(iota((Q, 128), 0), 9) == lax.div(iota((Q, 128), 1), 4), exact_dot(same, of_facet), 0.0)
+    load_map = jnp.where(
+        iota((Q, 128), 1) == 16, exact_dot(volume, push[0:Q]), exact_dot(lift, spread))
+    uh, ul = split(padded(load_map, QB))
+    uu[0:QB, :] = uh
+    uu[QB:2 * QB, :] = ul
+    arrive_pair(out2, rim2, 2)
+    put_table([rim2[0], rim2[1]], 8 * Q)
     for k in range(4):
         gather_rims(k)
-    change2 = change()
-    for copy in pair(wout, wrim, 4):
-        copy.wait_recv()
-    low, high_rim = rims(wrim)
-    far_w = jnp.concatenate([x[:, 256 * l:256 * l + 256] for x in (low, high_rim) for l in range(4)], axis=0)
+    result = s1[...] + push * w + scale * change()
+    arrive_pair(wout, wrim, 4)
+    far_w = jnp.concatenate([wrim[side, :, 256 * l:256 * l + 256] for side in range(2) for l in range(4)], axis=0)
     wh, wl = split(jnp.concatenate([own_w, far_w], axis=0))
     got = dot(jnp.concatenate([wh, wl], axis=0), hot[...])
     got = got[0:16] + got[16:32]
@@ -528,12 +546,10 @@
     nh, nl = split(jnp.concatenate(near, axis=0))
     first = dot(uu[...], nh)
     extra = first[0:QP] + first[QB:QB + QP] + dot(uu[0:QB, :], nl)[0:QP]
-    result = s1[...] + push * w + scale * (change2 + extra)
-    new_state_ref[...] = result[0:Q]
+    new_state_ref[...] = (result + scale * extra)[0:Q]
 
     for index, (outs, ins) in enumerate(((out1, rim1), (out2, rim2), (wout, wrim), (gout, grim))):
-        for copy in pair(outs, ins, 2 * index):
-            copy.wait_send()
+        sent_pair(outs, ins, 2 * index)
     for copy in edges(0) + edges(1):
         copy.wait_send()
     sent_all(cells_out, cells_in, cell_send, cell_recv)

time: 46.4 us -> 45.1 us (0.972)
  Pallas kernels: 44.4 us -> 43.5 us
    pallas_call x1, Pallas kernels: 43.6 us -> 42.7 us  [shards(): pl.pallas_call(kernel, out_shape=(pltpu.VMEM((Q, ELEMS), F32), pltpu.VMEM...]
where the time goes in v5:
time: 45.1 us; the launch traced here: 44.9 us
  Pallas kernels  43.5 us (96%)
  between operations  1.47 us (3%)
    pallas_call x1, Pallas kernels, shards(): pl.pallas_call(kernel, out_shape=(pltpu.VMEM((Q, ELEMS), F32), pltpu.VMEM...  42.7 us

profile of v5, /device:TPU:1, one launch (start us, length us, event | category | flops | bytes accessed | tf_op | source)
XLA Modules:
  0.0 44.9 jit_solution(4862278957732083783)
XLA Ops:
  1.3 42.7 %shard_map.184 = (f32[36,2048]{1,0:T(8,128)S(1)}, f32[128,128]{1,0:T(8,128)S(1)}, f32[128,128]{1,0:T(8,128)S(1)}) custom-call(f32[36,2048]{1,0:T(8,128)} %state_hbm.1, f32[1,2048]{1,0:T(1,128)} %bitcast.37, f32[36,36]{1,0:T(8,128)} %stiff_hbm.1, f32[36,36]{1,0:T(8,128)} %tmap_hbm.1, f32[36,36]{1,0:T(8,128)} %lift_hbm.1, s32[4,2048]{1,0:T(4,128)} %nel_hbm.1, ...), custom_call_target="tpu_custom_call" | custom-call | tf_op jit(solution)/shard_map/pallas_call | solution.py:639
  44.0 0.8 %shard_map.185 = (f32[36,2048]{1,0:T(8,128)}, f32[128,128]{1,0:T(8,128)}, f32[128,128]{1,0:T(8,128)}) custom-call(f32[36,2048]{1,0:T(8,128)S(1)} %get-tuple-element.9.refs_0_, f32[128,128]{1,0:T(8,128)S(1)} %get-tuple-element.10.refs_1_, f32[128,128]{1,0:T(8,128)S(1)} %get-tuple-element.11.refs_2_), custom_call_target="tpu_custom_call" | custom-call | tf_op jit(solution)/shard_map/pallas_call | solution.py:658

commit v6 on v5

--- a/solution.py
+++ b/solution.py
@@ -50,7 +50,10 @@
 
 
 def units(count, row):
-    return ones_where(iota((count, row.shape[1]), 0) == row).astype(BF16)
+    shape = (count, row.shape[1])
+    row = jnp.broadcast_to(row.astype(F32), (16, shape[1])).astype(BF16)
+    same = iota(shape, 0).astype(F32).astype(BF16) == jnp.concatenate([row] * (count // 16), axis=0)
+    return jnp.where(same, jnp.ones((), BF16), jnp.zeros((), BF16))
 
 
 def lanes(chunk, width=128):

time: 45.1 us -> 44.2 us (0.980)
  Pallas kernels: 43.5 us -> 42.6 us
    pallas_call x1, Pallas kernels: 42.7 us -> 41.8 us  [shards(): pl.pallas_call(kernel, out_shape=(pltpu.VMEM((Q, ELEMS), F32), pltpu.VMEM...]
where the time goes in v6:
time: 44.2 us; the launch traced here: 44 us
  Pallas kernels  42.6 us (96%)
  between operations  1.47 us (3%)
    pallas_call x1, Pallas kernels, shards(): pl.pallas_call(kernel, out_shape=(pltpu.VMEM((Q, ELEMS), F32), pltpu.VMEM...  41.8 us

profile of v6, /device:TPU:1, one launch (start us, length us, event | category | flops | bytes accessed | tf_op | source)
XLA Modules:
  0.0 44.0 jit_solution(11139598257375726954)
XLA Ops:
  1.3 41.8 %shard_map.184 = (f32[36,2048]{1,0:T(8,128)S(1)}, f32[128,128]{1,0:T(8,128)S(1)}, f32[128,128]{1,0:T(8,128)S(1)}) custom-call(f32[36,2048]{1,0:T(8,128)} %state_hbm.1, f32[1,2048]{1,0:T(1,128)} %bitcast.37, f32[36,36]{1,0:T(8,128)} %stiff_hbm.1, f32[36,36]{1,0:T(8,128)} %tmap_hbm.1, f32[36,36]{1,0:T(8,128)} %lift_hbm.1, s32[4,2048]{1,0:T(4,128)} %nel_hbm.1, ...), custom_call_target="tpu_custom_call" | custom-call | tf_op jit(solution)/shard_map/pallas_call | solution.py:642
  43.1 0.8 %shard_map.185 = (f32[36,2048]{1,0:T(8,128)}, f32[128,128]{1,0:T(8,128)}, f32[128,128]{1,0:T(8,128)}) custom-call(f32[36,2048]{1,0:T(8,128)S(1)} %get-tuple-element.9.refs_0_, f32[128,128]{1,0:T(8,128)S(1)} %get-tuple-element.10.refs_1_, f32[128,128]{1,0:T(8,128)S(1)} %get-tuple-element.11.refs_2_), custom_call_target="tpu_custom_call" | custom-call | tf_op jit(solution)/shard_map/pallas_call | solution.py:661
